TPU v7x, 128 devices: a whole 4x4x4 slice. The times are simulated.
128 devices in a mesh: gx: 32 (over x, z, y_lo), gy: 4 (over y_hi, core).
Axes of the slice: x: 4, y: 4 (y_hi: 2, y_lo: 2; y = y_hi * 2 + y_lo), z: 4, core: 2. Of those that a mesh axis runs over, the one named last changes fastest.
Arguments:
- source_snaps: float32 [4, 1536, 64, 256], P(None, 'gx', 'gy'), may hold values from -6 to 6
- receiver_snaps: float32 [4, 1536, 64, 256], P(None, 'gx', 'gy'), may hold values from -6 to 6
- snap_pairs: int32 [3, 2], replicated, may hold values from 0 to 3
- offset_lags: int32 [17], replicated, may hold values from -24 to 24, as said below
- weight_table: float32 [4, 17], replicated, may hold values from 0.2 to 1
- weight_index: int32 [3], replicated, may hold values from 0 to 3
Outputs:
- adjoint_source: float32 [3, 1536, 64, 256], P(None, 'gx', 'gy')
- adjoint_receiver: float32 [3, 1536, 64, 256], P(None, 'gx', 'gy')
Inputs may be any that keep to these rules, and one draw needn't show every extreme that they name: `offset_lags`: strictly increasing; the first entry is -24 and the last is 24.
All inputs are finite; a program needn't handle non-finite values.
Results may differ from a plain program's by a relative error of at most 0.00002.
Values sent between devices are 32-bit elements; how exact they have to be, the bound alone decides.
No kernel may reach another device: no remote copies, remote signals or barrier semaphores. Data moves between devices by JAX's collectives and lax.ppermute only.
A program may use at most 128 MiB of HBM per device.

v0:
```python
import functools

import jax
import jax.numpy as jnp
from jax import lax
from jax.experimental import pallas as pl
from jax.experimental.pallas import tpu as pltpu
from jax.sharding import PartitionSpec as P

F32 = jnp.float32
SMEM = pl.BlockSpec(memory_space=pltpu.SMEM)
VMEM = pl.BlockSpec(memory_space=pltpu.VMEM)
HBM = pl.BlockSpec(memory_space=pl.ANY)
MAIN = pl.BlockSpec(memory_space=pltpu.HBM)
SCOPED = 24 * 2**20

ODD, SECOND, COUNT, FIELD, SLOT, FIRST, ORDER, LAG = 0, 1, 2, 8, 16, 24, 32, 40


def moves(mesh):
    nx, ny = mesh.shape["gx"], mesh.shape["gy"]
    flat = lambda x, y: x * ny + y
    middle = list(range(1, ny - 1))
    across = [(x, x ^ 1) for x in range(nx) if x ^ 1 < nx]
    onward = [(x, x + 2) for x in range(0, nx - 2, 2)] + [(x, x - 2) for x in range(3, nx, 2)]
    whole = lambda route, rows: [(flat(a, y), flat(b, y)) for a, b in route for y in rows]
    seams = [(a, b) for y in range(1, ny - 1, 2) for a, b in ((y, y + 1), (y + 1, y))]
    return {
        "across": whole(across, range(ny)),
        "onward": whole(onward, range(ny)),
        "across_edge": whole(across, middle),
        "onward_edge": whole(onward, middle),
        "twins": [(flat(x, y), flat(x, y ^ 1)) for x in range(nx) for y in range(ny)],
        "seam": [(flat(x, a), flat(x, b)) for x in range(nx) for a, b in seams],
    }


def plan_kernel(snaps, pairs, lags, table, rows, plan, weights):
    units = 2 * pairs.shape[0]
    plan[ODD] = lax.rem(lax.axis_index("gx"), 2)
    plan[SECOND] = lax.rem(lax.axis_index("gy"), 2)
    ids = [pairs[u // 2, 1] if u % 2 == 0 else pairs[u // 2, 0] + snaps for u in range(units)]
    same = [[(ids[u] == ids[v]).astype(jnp.int32) for v in range(units)] for u in range(units)]
    uses = [sum(same[u]) for u in range(units)]
    leads = [jnp.int32(1)]
    for u in range(1, units):
        leads.append((sum(same[u][:u]) == 0).astype(jnp.int32))
    rank = []
    for u in range(units):
        ahead = jnp.int32(0)
        for v in range(units):
            if v != u:
                sooner = uses[v] >= uses[u] if v < u else uses[v] > uses[u]
                ahead = ahead + leads[v] * sooner.astype(jnp.int32)
        rank.append(ahead)
    slots = [sum(same[u][v] * leads[v] * rank[v] for v in range(units)) for u in range(units)]
    plan[COUNT] = sum(leads)
    for u in range(units):
        plan[SLOT + u] = slots[u]
        plan[FIELD + slots[u]] = ids[u]
        before = jnp.int32(0)
        for v in range(units):
            if v != u:
                sooner = slots[v] <= slots[u] if v < u else slots[v] < slots[u]
                before = before + sooner.astype(jnp.int32)
        plan[ORDER + before] = u
        plan[FIRST + u] = sum((slots[v] < u).astype(jnp.int32) for v in range(units))
    plan[FIRST + units] = units
    for h in range(lags.shape[0]):
        plan[LAG + h] = 2 * lags[h]
        for p in range(pairs.shape[0]):
            weights[p * lags.shape[0] + h] = table[rows[p], h]


def fetch(field, source, receiver, target, sem):
    snaps = receiver.shape[0]

    @pl.when(field < snaps)
    def _():
        pltpu.make_async_copy(receiver.at[jnp.minimum(field, snaps - 1)], target, sem).start()

    @pl.when(field >= snaps)
    def _():
        pltpu.make_async_copy(source.at[jnp.maximum(field - snaps, 0)], target, sem).start()

    return pltpu.make_async_copy(receiver.at[0], target, sem)


def lead_kernel(plan, source, receiver, out, sem):
    fetch(plan[FIELD], source, receiver, out, sem).wait()


def lead(plan, source, receiver):
    return pl.pallas_call(
        lead_kernel,
        out_shape=jax.ShapeDtypeStruct(source.shape[1:], F32),
        in_specs=[SMEM, HBM, HBM],
        out_specs=VMEM,
        scratch_shapes=[pltpu.SemaphoreType.DMA],
        compiler_params=pltpu.CompilerParams(vmem_limit_bytes=SCOPED),
        cost_estimate=pl.CostEstimate(flops=0, bytes_accessed=1600000, transcendentals=0),
    )(plan, source, receiver)


def gather_kernel(plan, source, receiver, fields, inner, outer, sems):
    count, cells, rows, _ = fields.shape
    waits = [fetch(plan[FIELD + s], source, receiver, fields.at[s], sems.at[s]) for s in range(count)]
    second = plan[SECOND] == 1
    for s, wait in enumerate(waits):
        wait.wait()

        def rim(x, carry):
            low, high = fields[s, x, 0:2], fields[s, x, rows - 2 : rows]
            inner[s, x] = jnp.where(second, low, high)
            outer[s, x] = jnp.where(second, high, low)
            return carry

        lax.fori_loop(0, cells, rim, 0, unroll=4)


def gather(plan, source, receiver, count):
    _, cells, rows, depth = source.shape
    edge = jax.ShapeDtypeStruct((count, cells, 2, depth), F32)
    return pl.pallas_call(
        gather_kernel,
        out_shape=[jax.ShapeDtypeStruct((count, cells, rows, depth), F32), edge, edge],
        in_specs=[SMEM, HBM, HBM],
        out_specs=[VMEM] * 3,
        scratch_shapes=[pltpu.SemaphoreType.DMA((count,))],
        compiler_params=pltpu.CompilerParams(vmem_limit_bytes=SCOPED),
        cost_estimate=pl.CostEstimate(flops=0, bytes_accessed=6000000, transcendentals=0),
    )(plan, source, receiver)


def take_kernel(slot, fields, *rest):
    out, sem = rest[-2:]
    copy = pltpu.make_async_copy(fields.at[slot], out, sem)
    copy.start()
    copy.wait()


def take(slot, fields, *earlier):
    return pl.pallas_call(
        functools.partial(take_kernel, slot),
        out_shape=jax.ShapeDtypeStruct(fields.shape[1:], F32),
        in_specs=[HBM] * (1 + len(earlier)),
        out_specs=VMEM,
        scratch_shapes=[pltpu.SemaphoreType.DMA],
        compiler_params=pltpu.CompilerParams(vmem_limit_bytes=SCOPED),
        cost_estimate=pl.CostEstimate(flops=0, bytes_accessed=1600000, transcendentals=0),
    )(fields, *earlier)


def cut_kernel(many, plan, *rest):
    blocks, inner = rest[:many], rest[-1]
    cells, rows, _ = blocks[0].shape
    second = plan[SECOND] == 1
    for i, block in enumerate(blocks):

        def rim(x, carry):
            inner[i, x] = jnp.where(second, block[x, 0:2], block[x, rows - 2 : rows])
            return carry

        lax.fori_loop(0, cells, rim, 0, unroll=4)


def cut(plan, blocks, earlier):
    cells, _, depth = blocks[0].shape
    return pl.pallas_call(
        functools.partial(cut_kernel, len(blocks)),
        out_shape=jax.ShapeDtypeStruct((len(blocks), cells, 2, depth), F32),
        in_specs=[SMEM] + [VMEM] * len(blocks) + [HBM] * len(earlier),
        out_specs=VMEM,
        compiler_params=pltpu.CompilerParams(vmem_limit_bytes=SCOPED),
        cost_estimate=pl.CostEstimate(flops=0, bytes_accessed=1000000, transcendentals=0),
    )(plan, *blocks, *earlier)


def image_kernel(
    slot, spot, plan, weights, fields, near, far, own_twin, own_edge, near_twin, near_edge, far_twin, far_edge, *rest
):
    to_source, to_receiver, token, ext, prod, mix, mext, done, sems = rest[-9:]
    _, cells, rows, depth = fields.shape
    halves = ext.shape[0]
    lanes = depth // halves
    pairs = to_source.shape[0]
    taps = weights.shape[0] // pairs
    odd, second = plan[ODD], plan[SECOND] == 1
    near_at = jnp.where(odd == 1, 0, 2 * cells)
    far_at = 2 * cells - near_at
    first, last = plan[FIRST + slot], plan[FIRST + slot + 1]
    part = [slice(z * lanes, (z + 1) * lanes) for z in range(halves)]
    low_tile = lax.broadcasted_iota(jnp.int32, (8, lanes), 0)

    def widen(target, at, block, twin, edge):
        def one(x, carry):
            for z in range(halves):
                t, e = twin[x, :, part[z]], edge[x, :, part[z]]
                target[z, at + x, 8 : rows + 8] = block[x, :, part[z]]
                target[z, at + x, 6:8] = jnp.where(second, t, e)
                target[z, at + x, rows + 8 : rows + 10] = jnp.where(second, e, t)
            return carry

        lax.fori_loop(0, cells, one, 0, unroll=4)

    widen(ext, cells, fields.at[slot], own_twin.at[slot], own_edge.at[slot])
    widen(ext, near_at, near, near_twin.at[0], near_edge.at[slot])
    widen(ext, far_at, far, far_twin.at[spot], far_edge.at[slot])

    def product(x, carry):
        for z in range(halves):
            e, q = ext.at[z, x], prod.at[z, x]
            here = e[8 : rows + 8]
            q[0:rows] = here * here
            q[rows : 2 * rows] = here * e[9 : rows + 9]
            q[2 * rows : 3 * rows] = here * e[10 : rows + 10]
            base = e[0:8]
            one = base * e[1:9]
            two = base * e[2:10]
            q[3 * rows : 3 * rows + 8] = jnp.where(low_tile >= 6, two, pltpu.roll(one, 6, 0))
        return carry

    lax.fori_loop(0, 3 * cells, product, 0, unroll=4)

    def unit(index, carry):
        i = index - first
        u = plan[ORDER + index]
        to_r = lax.rem(u, 2)
        p = lax.div(u, 2)
        mate = plan[SLOT + u + 1 - 2 * to_r]
        sign = 1 - 2 * to_r
        at = [cells + sign * plan[LAG + h] for h in range(taps)]
        scale = [weights[p * taps + h] for h in range(taps)]
        widen(mext, 0, fields.at[mate], own_twin.at[mate], own_edge.at[mate])

        def total(x, carry):
            for z in range(halves):
                m, s = mix.at[z], mext.at[z, x]
                acc = None
                for h in range(taps):
                    term = scale[h] * prod[z, x + at[h]]
                    acc = term if acc is None else acc + term
                m[0, 8 : rows + 8] = acc[rows : 2 * rows]
                m[1, 8 : rows + 8] = acc[2 * rows : 3 * rows]
                extra = acc[3 * rows : 3 * rows + 8]
                m[0, 0:8] = pltpu.roll(extra, 2, 0)
                m[1, 0:8] = extra
                one = acc[rows : 2 * rows] * s[9 : rows + 9] + m[0, 7 : rows + 7] * s[7 : rows + 7]
                two = acc[2 * rows : 3 * rows] * s[10 : rows + 10] + m[1, 6 : rows + 6] * s[6 : rows + 6]
                done[i, x, :, part[z]] = 0.375 * (acc[0:rows] * s[8 : rows + 8]) + 0.25 * one + 0.0625 * two
            return carry

        lax.fori_loop(0, cells, total, 0)
        for which, target in enumerate((to_source, to_receiver)):

            @pl.when(to_r == which)
            def _():
                pltpu.make_async_copy(done.at[i], target.at[p], sems.at[i]).start()

        return carry

    lax.fori_loop(first, last, unit, 0)

    def settle(index, carry):
        i = index - first
        pltpu.make_async_copy(done.at[i], to_source.at[0], sems.at[i]).wait()
        return carry

    lax.fori_loop(first, last, settle, 0)
    token[...] = jnp.zeros_like(token)


def image(slot, pairs, plan, weights, fields, near, far, halos, spot, outs):
    _, cells, rows, depth = fields.shape
    whole = jax.ShapeDtypeStruct((pairs, cells, rows, depth), F32)
    halves = 2
    lanes = depth // halves
    return pl.pallas_call(
        functools.partial(image_kernel, slot, spot),
        out_shape=[whole, whole, jax.ShapeDtypeStruct((8, 128), F32)],
        in_specs=[SMEM] * 2 + [VMEM] * 9 + [MAIN] * len(outs),
        out_specs=[MAIN, MAIN, VMEM],
        input_output_aliases={11 + i: i for i in range(len(outs))},
        scratch_shapes=[
            pltpu.VMEM((halves, 3 * cells, rows + 16, lanes), F32),
            pltpu.VMEM((halves, 3 * cells, 3 * rows + 8, lanes), F32),
            pltpu.VMEM((halves, 2, rows + 8, lanes), F32),
            pltpu.VMEM((halves, cells, rows + 16, lanes), F32),
            pltpu.VMEM((pairs, cells, rows, depth), F32),
            pltpu.SemaphoreType.DMA((pairs,)),
        ],
        compiler_params=pltpu.CompilerParams(vmem_limit_bytes=SCOPED),
        cost_estimate=pl.CostEstimate(flops=22 * 10**6, bytes_accessed=22 * 10**6, transcendentals=0),
    )(plan, weights, fields, near, far, *halos, *outs)


def work(count, pairs, routes, plan, weights, source, receiver):
    send = lambda value, route: lax.ppermute(value, ("gx", "gy"), routes[route])

    near = [send(lead(plan, source, receiver), "across")]
    fields, inner, outer = gather(plan, source, receiver, count)
    own_twin = send(inner, "twins")
    own_edge = send(outer, "seam")
    near.append(send(take(1, fields), "across"))
    near_edge = send(own_edge, "across_edge")
    far_edge = send(near_edge, "onward_edge")

    far, twins, tokens = [], [], []
    outs = ()
    for s in range(count + 1):
        if s < count:
            far.append(send(near[s], "onward"))
            if s + 2 < count:
                earlier = [near[s], own_twin, own_edge] if s == 0 else [near[s], far[s - 1], near_edge, twins[s - 1]]
                earlier = earlier + tokens[s - 2 : s - 1] if s >= 2 else earlier
                near.append(send(take(s + 2, fields, *earlier), "across"))
        blocks = near[s : s + 1] + (far[s - 1 : s] if s >= 1 else [])
        twins.append(send(cut(plan, blocks, tokens[s - 2 : s - 1] if s >= 2 else []), "twins"))
        if s >= 1:
            halos = (own_twin, own_edge, twins[s - 1], near_edge, twins[s], far_edge)
            *outs, token = image(s - 1, pairs, plan, weights, fields, near[s - 1], far[s - 1], halos, len(blocks) - 1, outs)
            tokens.append(token)
    return tuple(outs)


def local(routes, source_snaps, receiver_snaps, snap_pairs, offset_lags, weight_table, weight_index):
    pairs = snap_pairs.shape[0]
    plan, weights = pl.pallas_call(
        functools.partial(plan_kernel, receiver_snaps.shape[0]),
        out_shape=[
            jax.ShapeDtypeStruct((LAG + offset_lags.shape[0],), jnp.int32),
            jax.ShapeDtypeStruct((pairs * offset_lags.shape[0],), F32),
        ],
        in_specs=[SMEM] * 4,
        out_specs=[SMEM] * 2,
    )(snap_pairs, offset_lags, weight_table, weight_index)
    least = 2
    most = 2 * pairs
    branches = [functools.partial(work, count, pairs, routes) for count in range(least, most + 1)]
    return lax.switch(plan[COUNT] - least, branches, plan, weights, source_snaps, receiver_snaps)


def solution(mesh):
    routes = moves(mesh)
    split = P(None, "gx", "gy", None)
    return jax.shard_map(
        functools.partial(local, routes),
        mesh=mesh,
        in_specs=(split, split, P(), P(), P(), P()),
        out_specs=(split, split),
        check_vma=False,
    )
```

profile of v0, /device:TPU:7, one launch (start us, length us, event | category | flops | bytes accessed | tf_op | source)
XLA Modules:
  0.0 158.6 jit_solution(9836251527960805231)
XLA Ops:
  0.6 1.3 copy.38.pairs
  2.0 1.6 %shard_map.77 = (s32[57]{0:T(128)S(1)}, f32[51]{0:T(128)S(1)}) custom-call(s32[3,2]{1,0:T(4,128)} %copy.38.pairs, s32[17]{0:T(128)} %lags.1, f32[4,17]{1,0:T(4,128)} %table.1, s32[3]{0:T(128)} %rows.1), custom_call_target="tpu_custom_call" | custom-call | tf_op jit(solution)/shard_map/pallas_call | solution.py:328
  3.6 0.6 slice.3
  4.8 153.8 %conditional.1 = (f32[3,48,16,256]{3,2,1,0:T(8,128)}, f32[3,48,16,256]{3,2,1,0:T(8,128)}) conditional(s32[]{:T(128)} %bitcast, (s32[57]{0:T(128)S(1)}, f32[4,48,16,256]{3,2,1,0:T(8,128)}, f32[4,48,16,256]{3,2,1,0:T(8,128)}, f32[51]{0:T(128)S(1)}) %tuple.27, (s32[57]{0:T(128)S(1)}, f32[4,48,16,256]{3,2,1,0:T(8,128)}, ...), branch_computations={%region_0.0_spmd, %region_1.0_spmd, %region_2.0_spmd, %region_3.0_... | conditional | flops 132000000 | bytes 250545744 | solution.py:340
  4.8 0.0 copy-start.12
  4.9 0.0 copy-start.17
  4.9 2.0 %branch_2_fun.16 = f32[48,16,256]{2,1,0:T(8,128)S(1)} custom-call(s32[57]{0:T(128)S(1)} %get-tuple-element.67.plan, f32[4,48,16,256]{3,2,1,0:T(8,128)} %get-tuple-element.69.source, f32[4,48,16,256]{3,2,1,0:T(8,128)} %get-tuple-element.70.receiver), custom_call_target="tpu_custom_call" | custom-call | bytes 1600000 | tf_op jit(solution)/shard_map/cond/branch_2_fun/pallas_call | solution.py:94
  6.8 1.4 collective-permute-start.26
  8.2 0.0 copy-done.12
  8.2 0.0 copy-done.17
  8.2 1.5 branch_2_fun.14
  9.7 0.1 branch_2_fun.15
  9.8 1.1 collective-permute-start.25
  10.9 5.4 %collective-permute-start.28 = (f32[4,48,2,256]{3,2,1,0:T(2,128)S(1)}, f32[4,48,2,256]{3,2,1,0:T(2,128)S(1)}, u32[]{:S(2)}, u32[]{:S(2)}) collective-permute-start(f32[4,48,2,256]{3,2,1,0:T(2,128)S(1)} %get-tuple-element.72), channel_id=1, source_target_pairs={{1,2},{2,1},{5,6},{6,5},{9,10},{10,9},{13,14},{14,13},{17,18},{18,... | collective-permute-start | bytes 1179656 | tf_op jit(solution)/shard_map/cond/branch_2_fun/ppermute | solution.py:298
  16.2 9.1 %collective-permute-done.26.rest_0_.near = f32[48,16,256]{2,1,0:T(8,128)S(1)} collective-permute-done((f32[48,16,256]{2,1,0:T(8,128)S(1)}, f32[48,16,256]{2,1,0:T(8,128)S(1)}, u32[]{:S(2)}, u32[]{:S(2)}) %collective-permute-start.26) | collective-permute-done | bytes 786464 | tf_op jit(solution)/shard_map/cond/branch_2_fun/ppermute | solution.py:298
  25.3 3.5 %collective-permute-start.27 = (f32[48,16,256]{2,1,0:T(8,128)S(1)}, f32[48,16,256]{2,1,0:T(8,128)S(1)}, u32[]{:S(2)}, u32[]{:S(2)}) collective-permute-start(f32[48,16,256]{2,1,0:T(8,128)S(1)} %collective-permute-done.26.rest_0_.near), channel_id=1, source_target_pairs={{0,8},{1,9},{2,10},{3,11},{8,16},{9,17},{10,18},{11,19},{16,24},{1... | collective-permute-start | bytes 2359304 | tf_op jit(solution)/shard_map/cond/branch_2_fun/ppermute | solution.py:298
  28.9 3.1 %collective-permute-start.33 = (f32[4,48,2,256]{3,2,1,0:T(2,128)S(1)}, f32[4,48,2,256]{3,2,1,0:T(2,128)S(1)}, u32[]{:S(2)}, u32[]{:S(2)}) collective-permute-start(f32[4,48,2,256]{3,2,1,0:T(2,128)S(1)} %get-tuple-element.73), channel_id=1, source_target_pairs={{0,1},{1,0},{2,3},{3,2},{4,5},{5,4},{6,7},{7,6},{8,9},{9,8},{10,11... | collective-permute-start | bytes 1179656 | tf_op jit(solution)/shard_map/cond/branch_2_fun/ppermute | solution.py:298
  31.9 23.1 %collective-permute-done.28.rest_2_.own_edge = f32[4,48,2,256]{3,2,1,0:T(2,128)S(1)} collective-permute-done((f32[4,48,2,256]{3,2,1,0:T(2,128)S(1)}, f32[4,48,2,256]{3,2,1,0:T(2,128)S(1)}, u32[]{:S(2)}, u32[]{:S(2)}) %collective-permute-start.28) | collective-permute-done | bytes 393248 | tf_op jit(solution)/shard_map/cond/branch_2_fun/ppermute | solution.py:298
  55.1 1.9 %collective-permute-start.29 = (f32[4,48,2,256]{3,2,1,0:T(2,128)S(1)}, f32[4,48,2,256]{3,2,1,0:T(2,128)S(1)}, u32[]{:S(2)}, u32[]{:S(2)}) collective-permute-start(f32[4,48,2,256]{3,2,1,0:T(2,128)S(1)} %collective-permute-done.28.rest_2_.own_edge), channel_id=1, source_target_pairs={{1,5},{2,6},{5,1},{6,2},{9,13},{10,14},{13,9},{14,10},{17,21},{18,... | collective-permute-start | bytes 1179656 | tf_op jit(solution)/shard_map/cond/branch_2_fun/ppermute | solution.py:298
  57.0 0.0 collective-permute-done.33.rest_1_.own_twin
  57.0 0.1 branch_2_fun.19
  57.1 1.5 collective-permute-start.34
  58.6 0.6 branch_2_fun.17
  59.3 0.1 collective-permute-start.30
  59.4 0.0 collective-permute-done.25.rest_0_.near
  59.4 4.2 %collective-permute-done.29.rest_2_.near_edge = f32[4,48,2,256]{3,2,1,0:T(2,128)S(1)} collective-permute-done((f32[4,48,2,256]{3,2,1,0:T(2,128)S(1)}, f32[4,48,2,256]{3,2,1,0:T(2,128)S(1)}, u32[]{:S(2)}, u32[]{:S(2)}) %collective-permute-start.29) | collective-permute-done | bytes 393248 | tf_op jit(solution)/shard_map/cond/branch_2_fun/ppermute | solution.py:298
  63.6 0.0 collective-permute-done.30.rest_3_.near_twin
  63.6 0.0 collective-permute-done.27.rest_1_.far
  63.6 0.1 branch_2_fun.18
  63.7 0.1 collective-permute-start.31
  63.8 3.5 %collective-permute-start.36 = (f32[48,16,256]{2,1,0:T(8,128)S(1)}, f32[48,16,256]{2,1,0:T(8,128)S(1)}, u32[]{:S(2)}, u32[]{:S(2)}) collective-permute-start(f32[48,16,256]{2,1,0:T(8,128)S(1)} %collective-permute-done.25.rest_0_.near), channel_id=1, source_target_pairs={{0,8},{1,9},{2,10},{3,11},{8,16},{9,17},{10,18},{11,19},{16,24},{1... | collective-permute-start | bytes 2359304 | tf_op jit(solution)/shard_map/cond/branch_2_fun/ppermute | solution.py:298
  67.3 13.1 %collective-permute-done.34.rest_0_.near = f32[48,16,256]{2,1,0:T(8,128)S(1)} collective-permute-done((f32[48,16,256]{2,1,0:T(8,128)S(1)}, f32[48,16,256]{2,1,0:T(8,128)S(1)}, u32[]{:S(2)}, u32[]{:S(2)}) %collective-permute-start.34) | collective-permute-done | bytes 786464 | tf_op jit(solution)/shard_map/cond/branch_2_fun/ppermute | solution.py:298
  80.4 3.5 %collective-permute-start.35 = (f32[48,16,256]{2,1,0:T(8,128)S(1)}, f32[48,16,256]{2,1,0:T(8,128)S(1)}, u32[]{:S(2)}, u32[]{:S(2)}) collective-permute-start(f32[48,16,256]{2,1,0:T(8,128)S(1)} %collective-permute-done.34.rest_0_.near), channel_id=1, source_target_pairs={{0,8},{1,9},{2,10},{3,11},{8,16},{9,17},{10,18},{11,19},{16,24},{1... | collective-permute-start | bytes 2359304 | tf_op jit(solution)/shard_map/cond/branch_2_fun/ppermute | solution.py:298
  84.0 3.5 %collective-permute-start.38 = (f32[4,48,2,256]{3,2,1,0:T(2,128)S(1)}, f32[4,48,2,256]{3,2,1,0:T(2,128)S(1)}, u32[]{:S(2)}, u32[]{:S(2)}) collective-permute-start(f32[4,48,2,256]{3,2,1,0:T(2,128)S(1)} %collective-permute-done.29.rest_2_.near_edge), channel_id=1, source_target_pairs={{1,9},{2,10},{9,17},{10,18},{17,25},{18,26},{25,33},{26,34},{33,41... | collective-permute-start | bytes 1179656 | tf_op jit(solution)/shard_map/cond/branch_2_fun/ppermute | solution.py:298
  87.5 1.6 %collective-permute-done.31.rest_0_.near = f32[48,16,256]{2,1,0:T(8,128)S(1)} collective-permute-done((f32[48,16,256]{2,1,0:T(8,128)S(1)}, f32[48,16,256]{2,1,0:T(8,128)S(1)}, u32[]{:S(2)}, u32[]{:S(2)}) %collective-permute-start.31) | collective-permute-done | bytes 786464 | tf_op jit(solution)/shard_map/cond/branch_2_fun/ppermute | solution.py:298
  89.2 3.5 %collective-permute-start.32 = (f32[48,16,256]{2,1,0:T(8,128)S(1)}, f32[48,16,256]{2,1,0:T(8,128)S(1)}, u32[]{:S(2)}, u32[]{:S(2)}) collective-permute-start(f32[48,16,256]{2,1,0:T(8,128)S(1)} %collective-permute-done.31.rest_0_.near), channel_id=1, source_target_pairs={{0,8},{1,9},{2,10},{3,11},{8,16},{9,17},{10,18},{11,19},{16,24},{1... | collective-permute-start | bytes 2359304 | tf_op jit(solution)/shard_map/cond/branch_2_fun/ppermute | solution.py:298
  92.7 0.8 branch_2_fun.20
  93.5 0.1 collective-permute-start.37
  93.6 19.6 %collective-permute-done.38.far_edge = f32[4,48,2,256]{3,2,1,0:T(2,128)S(1)} collective-permute-done((f32[4,48,2,256]{3,2,1,0:T(2,128)S(1)}, f32[4,48,2,256]{3,2,1,0:T(2,128)S(1)}, u32[]{:S(2)}, u32[]{:S(2)}) %collective-permute-start.38) | collective-permute-done | bytes 393248 | tf_op jit(solution)/shard_map/cond/branch_2_fun/ppermute | solution.py:298
  113.1 0.0 collective-permute-done.37.far_twin.near_twin
  113.1 11.4 %branch_2_fun.21 = (f32[3,48,16,256]{3,2,1,0:T(8,128)S(1)}, f32[3,48,16,256]{3,2,1,0:T(8,128)S(1)}, f32[8,128]{1,0:T(8,128)S(1)}) custom-call(s32[57]{0:T(128)S(1)} %get-tuple-element.67.plan, f32[51]{0:T(128)S(1)} %get-tuple-element.68.weights, f32[4,48,16,256]{3,2,1,0:T(8,128)S(1)} %get-tuple-element.71.fields, ...), custom_call_target="tpu_custom_call" | custom-call | flops 22000000 | bytes 22000000 | tf_op jit(solution)/shard_map/cond/branch_2_fun/pallas_call | solution.py:278
  124.5 0.0 collective-permute-done.36.rest_1_.far
  124.5 0.8 branch_2_fun.22
  125.3 0.1 collective-permute-start.39
  125.4 1.4 collective-permute-done.39.far_twin.near_twin
  126.8 11.4 %branch_2_fun.23 = (f32[3,48,16,256]{3,2,1,0:T(8,128)S(1)}, f32[3,48,16,256]{3,2,1,0:T(8,128)S(1)}, f32[8,128]{1,0:T(8,128)S(1)}) custom-call(s32[57]{0:T(128)S(1)} %get-tuple-element.67.plan, f32[51]{0:T(128)S(1)} %get-tuple-element.68.weights, f32[4,48,16,256]{3,2,1,0:T(8,128)S(1)} %get-tuple-element.71.fields, ...), custom_call_target="tpu_custom_call", output_to_operand_aliasing={{0}: (11, {}), {1}: (12, {})} | custom-call | flops 22000000 | bytes 22000000 | tf_op jit(solution)/shard_map/cond/branch_2_fun/pallas_call | solution.py:278
  138.2 0.0 collective-permute-done.35.rest_1_.far
  138.2 0.8 branch_2_fun.24
  139.0 0.2 collective-permute-start.40
  139.2 1.3 collective-permute-done.40.far_twin.near_twin
  140.5 6.6 %branch_2_fun.25 = (f32[3,48,16,256]{3,2,1,0:T(8,128)S(1)}, f32[3,48,16,256]{3,2,1,0:T(8,128)S(1)}, f32[8,128]{1,0:T(8,128)S(1)}) custom-call(s32[57]{0:T(128)S(1)} %get-tuple-element.67.plan, f32[51]{0:T(128)S(1)} %get-tuple-element.68.weights, f32[4,48,16,256]{3,2,1,0:T(8,128)S(1)} %get-tuple-element.71.fields, ...), custom_call_target="tpu_custom_call", output_to_operand_aliasing={{0}: (11, {}), {1}: (12, {})} | custom-call | flops 22000000 | bytes 22000000 | tf_op jit(solution)/shard_map/cond/branch_2_fun/pallas_call | solution.py:278
  147.1 0.0 collective-permute-done.32.rest_0_.far
  147.2 0.6 branch_2_fun.26
  147.8 0.2 collective-permute-start.41
  148.0 1.2 collective-permute-done.41.far_twin
  149.2 7.2 %branch_2_fun.27 = (f32[3,48,16,256]{3,2,1,0:T(8,128)S(1)}, f32[3,48,16,256]{3,2,1,0:T(8,128)S(1)}, f32[8,128]{1,0:T(8,128)}) custom-call(s32[57]{0:T(128)S(1)} %get-tuple-element.67.plan, f32[51]{0:T(128)S(1)} %get-tuple-element.68.weights, f32[4,48,16,256]{3,2,1,0:T(8,128)S(1)} %get-tuple-element.71.fields, ...), custom_call_target="tpu_custom_call", output_to_operand_aliasing={{0}: (11, {}), {1}: (12, {})} | custom-call | flops 22000000 | bytes 22000000 | tf_op jit(solution)/shard_map/cond/branch_2_fun/pallas_call | solution.py:278
  156.4 0.0 copy-start.2
  156.4 0.0 copy-start.7
  156.4 1.4 copy-done.2
  157.8 0.8 copy-done.7
Async XLA Ops:
  4.8 3.4 %copy-start.12 = (f32[4,48,16,256]{3,2,1,0:T(8,128)S(1)}, f32[4,48,16,256]{3,2,1,0:T(8,128)}, u32[]{:S(2)}) copy-start(f32[4,48,16,256]{3,2,1,0:T(8,128)} %get-tuple-element.69.source) | copy-start | bytes 9437188 | tf_op jit(solution)/shard_map/cond
  4.9 3.4 %copy-start.17 = (f32[4,48,16,256]{3,2,1,0:T(8,128)S(1)}, f32[4,48,16,256]{3,2,1,0:T(8,128)}, u32[]{:S(2)}) copy-start(f32[4,48,16,256]{3,2,1,0:T(8,128)} %get-tuple-element.70.receiver) | copy-start | bytes 9437188 | tf_op jit(solution)/shard_map/cond
  6.8 18.5 %collective-permute-start.26 = (f32[48,16,256]{2,1,0:T(8,128)S(1)}, f32[48,16,256]{2,1,0:T(8,128)S(1)}, u32[]{:S(2)}, u32[]{:S(2)}) collective-permute-start(f32[48,16,256]{2,1,0:T(8,128)S(1)} %branch_2_fun.16), channel_id=1, source_target_pairs={{0,4},{1,5},{2,6},{3,7},{4,0},{5,1},{6,2},{7,3},{8,12},{9,13},{10,... | collective-permute-start | bytes 2359304 | tf_op jit(solution)/shard_map/cond/branch_2_fun/ppermute | solution.py:298
  9.8 49.6 %collective-permute-start.25 = (f32[48,16,256]{2,1,0:T(8,128)S(1)}, f32[48,16,256]{2,1,0:T(8,128)S(1)}, u32[]{:S(2)}, u32[]{:S(2)}) collective-permute-start(f32[48,16,256]{2,1,0:T(8,128)S(1)} %branch_2_fun.15), channel_id=1, source_target_pairs={{0,4},{1,5},{2,6},{3,7},{4,0},{5,1},{6,2},{7,3},{8,12},{9,13},{10,... | collective-permute-start | bytes 2359304 | tf_op jit(solution)/shard_map/cond/branch_2_fun/ppermute | solution.py:298
  10.9 44.2 %collective-permute-start.28 = (f32[4,48,2,256]{3,2,1,0:T(2,128)S(1)}, f32[4,48,2,256]{3,2,1,0:T(2,128)S(1)}, u32[]{:S(2)}, u32[]{:S(2)}) collective-permute-start(f32[4,48,2,256]{3,2,1,0:T(2,128)S(1)} %get-tuple-element.72), channel_id=1, source_target_pairs={{1,2},{2,1},{5,6},{6,5},{9,10},{10,9},{13,14},{14,13},{17,18},{18,... | collective-permute-start | bytes 1179656 | tf_op jit(solution)/shard_map/cond/branch_2_fun/ppermute | solution.py:298
  25.3 38.3 %collective-permute-start.27 = (f32[48,16,256]{2,1,0:T(8,128)S(1)}, f32[48,16,256]{2,1,0:T(8,128)S(1)}, u32[]{:S(2)}, u32[]{:S(2)}) collective-permute-start(f32[48,16,256]{2,1,0:T(8,128)S(1)} %collective-permute-done.26.rest_0_.near), channel_id=1, source_target_pairs={{0,8},{1,9},{2,10},{3,11},{8,16},{9,17},{10,18},{11,19},{16,24},{1... | collective-permute-start | bytes 2359304 | tf_op jit(solution)/shard_map/cond/branch_2_fun/ppermute | solution.py:298
  28.9 28.1 %collective-permute-start.33 = (f32[4,48,2,256]{3,2,1,0:T(2,128)S(1)}, f32[4,48,2,256]{3,2,1,0:T(2,128)S(1)}, u32[]{:S(2)}, u32[]{:S(2)}) collective-permute-start(f32[4,48,2,256]{3,2,1,0:T(2,128)S(1)} %get-tuple-element.73), channel_id=1, source_target_pairs={{0,1},{1,0},{2,3},{3,2},{4,5},{5,4},{6,7},{7,6},{8,9},{9,8},{10,11... | collective-permute-start | bytes 1179656 | tf_op jit(solution)/shard_map/cond/branch_2_fun/ppermute | solution.py:298
  55.1 8.5 %collective-permute-start.29 = (f32[4,48,2,256]{3,2,1,0:T(2,128)S(1)}, f32[4,48,2,256]{3,2,1,0:T(2,128)S(1)}, u32[]{:S(2)}, u32[]{:S(2)}) collective-permute-start(f32[4,48,2,256]{3,2,1,0:T(2,128)S(1)} %collective-permute-done.28.rest_2_.own_edge), channel_id=1, source_target_pairs={{1,5},{2,6},{5,1},{6,2},{9,13},{10,14},{13,9},{14,10},{17,21},{18,... | collective-permute-start | bytes 1179656 | tf_op jit(solution)/shard_map/cond/branch_2_fun/ppermute | solution.py:298
  57.1 23.3 %collective-permute-start.34 = (f32[48,16,256]{2,1,0:T(8,128)S(1)}, f32[48,16,256]{2,1,0:T(8,128)S(1)}, u32[]{:S(2)}, u32[]{:S(2)}) collective-permute-start(f32[48,16,256]{2,1,0:T(8,128)S(1)} %branch_2_fun.19), channel_id=1, source_target_pairs={{0,4},{1,5},{2,6},{3,7},{4,0},{5,1},{6,2},{7,3},{8,12},{9,13},{10,... | collective-permute-start | bytes 2359304 | tf_op jit(solution)/shard_map/cond/branch_2_fun/ppermute | solution.py:298
  59.3 4.3 %collective-permute-start.30 = (f32[1,48,2,256]{3,2,1,0:T(2,128)S(1)}, f32[1,48,2,256]{3,2,1,0:T(2,128)S(1)}, u32[]{:S(2)}, u32[]{:S(2)}) collective-permute-start(f32[1,48,2,256]{3,2,1,0:T(2,128)S(1)} %branch_2_fun.17), channel_id=1, source_target_pairs={{0,1},{1,0},{2,3},{3,2},{4,5},{5,4},{6,7},{7,6},{8,9},{9,8},{10,11... | collective-permute-start | bytes 294920 | tf_op jit(solution)/shard_map/cond/branch_2_fun/ppermute | solution.py:298
  63.7 25.5 %collective-permute-start.31 = (f32[48,16,256]{2,1,0:T(8,128)S(1)}, f32[48,16,256]{2,1,0:T(8,128)S(1)}, u32[]{:S(2)}, u32[]{:S(2)}) collective-permute-start(f32[48,16,256]{2,1,0:T(8,128)S(1)} %branch_2_fun.18), channel_id=1, source_target_pairs={{0,4},{1,5},{2,6},{3,7},{4,0},{5,1},{6,2},{7,3},{8,12},{9,13},{10,... | collective-permute-start | bytes 2359304 | tf_op jit(solution)/shard_map/cond/branch_2_fun/ppermute | solution.py:298
  63.8 60.8 %collective-permute-start.36 = (f32[48,16,256]{2,1,0:T(8,128)S(1)}, f32[48,16,256]{2,1,0:T(8,128)S(1)}, u32[]{:S(2)}, u32[]{:S(2)}) collective-permute-start(f32[48,16,256]{2,1,0:T(8,128)S(1)} %collective-permute-done.25.rest_0_.near), channel_id=1, source_target_pairs={{0,8},{1,9},{2,10},{3,11},{8,16},{9,17},{10,18},{11,19},{16,24},{1... | collective-permute-start | bytes 2359304 | tf_op jit(solution)/shard_map/cond/branch_2_fun/ppermute | solution.py:298
  80.4 57.8 %collective-permute-start.35 = (f32[48,16,256]{2,1,0:T(8,128)S(1)}, f32[48,16,256]{2,1,0:T(8,128)S(1)}, u32[]{:S(2)}, u32[]{:S(2)}) collective-permute-start(f32[48,16,256]{2,1,0:T(8,128)S(1)} %collective-permute-done.34.rest_0_.near), channel_id=1, source_target_pairs={{0,8},{1,9},{2,10},{3,11},{8,16},{9,17},{10,18},{11,19},{16,24},{1... | collective-permute-start | bytes 2359304 | tf_op jit(solution)/shard_map/cond/branch_2_fun/ppermute | solution.py:298
  84.0 29.2 %collective-permute-start.38 = (f32[4,48,2,256]{3,2,1,0:T(2,128)S(1)}, f32[4,48,2,256]{3,2,1,0:T(2,128)S(1)}, u32[]{:S(2)}, u32[]{:S(2)}) collective-permute-start(f32[4,48,2,256]{3,2,1,0:T(2,128)S(1)} %collective-permute-done.29.rest_2_.near_edge), channel_id=1, source_target_pairs={{1,9},{2,10},{9,17},{10,18},{17,25},{18,26},{25,33},{26,34},{33,41... | collective-permute-start | bytes 1179656 | tf_op jit(solution)/shard_map/cond/branch_2_fun/ppermute | solution.py:298
  89.2 58.0 %collective-permute-start.32 = (f32[48,16,256]{2,1,0:T(8,128)S(1)}, f32[48,16,256]{2,1,0:T(8,128)S(1)}, u32[]{:S(2)}, u32[]{:S(2)}) collective-permute-start(f32[48,16,256]{2,1,0:T(8,128)S(1)} %collective-permute-done.31.rest_0_.near), channel_id=1, source_target_pairs={{0,8},{1,9},{2,10},{3,11},{8,16},{9,17},{10,18},{11,19},{16,24},{1... | collective-permute-start | bytes 2359304 | tf_op jit(solution)/shard_map/cond/branch_2_fun/ppermute | solution.py:298
  93.5 19.7 %collective-permute-start.37 = (f32[2,48,2,256]{3,2,1,0:T(2,128)S(1)}, f32[2,48,2,256]{3,2,1,0:T(2,128)S(1)}, u32[]{:S(2)}, u32[]{:S(2)}) collective-permute-start(f32[2,48,2,256]{3,2,1,0:T(2,128)S(1)} %branch_2_fun.20), channel_id=1, source_target_pairs={{0,1},{1,0},{2,3},{3,2},{4,5},{5,4},{6,7},{7,6},{8,9},{9,8},{10,11... | collective-permute-start | bytes 589832 | tf_op jit(solution)/shard_map/cond/branch_2_fun/ppermute | solution.py:298
  125.3 1.5 collective-permute-start.39
  139.0 1.5 collective-permute-start.40
  147.8 1.4 collective-permute-start.41
  156.4 1.4 copy-start.2
  156.4 2.2 %copy-start.7 = (f32[3,48,16,256]{3,2,1,0:T(8,128)}, f32[3,48,16,256]{3,2,1,0:T(8,128)S(1)}, u32[]{:S(2)}) copy-start(f32[3,48,16,256]{3,2,1,0:T(8,128)S(1)} %get-tuple-element.141) | copy-start | bytes 7077892 | tf_op jit(solution)/shard_map/cond
where the time goes:
time: 158 us; the launch traced here: 159 us
  waiting for transfers between devices  74.7 us (47%)
  Pallas kernels  45.4 us (29%)
  starting transfers between devices  32.8 us (21%)
  local copies, waits for them, and re-layouts  4.1 us (3%)
    ppermute x17, waiting for transfers between devices, work(): send = lambda value, route: lax.ppermute(value, ('gx', 'gy'), routes[route])  74.7 us
    pallas_call x4, Pallas kernels, image(): pl.pallas_call(functools.partial(image_kernel, slot, spot), out_shape=[wh...  36.6 us
    ppermute x17, starting transfers between devices, work(): send = lambda value, route: lax.ppermute(value, ('gx', 'gy'), routes[route])  32.8 us
    pallas_call x5, Pallas kernels, cut(): pl.pallas_call(functools.partial(cut_kernel, len(blocks)), out_shape=jax....  3.57 us
  transfers between devices with their start and end apart: 17, of which 9 were waited for; matrix products, arithmetic and copies ran while one was open for 0% of the time, Pallas kernels for 21%

commit v1 on v0

--- a/solution.py
+++ b/solution.py
@@ -20,7 +20,6 @@
 def moves(mesh):
     nx, ny = mesh.shape["gx"], mesh.shape["gy"]
     flat = lambda x, y: x * ny + y
-    middle = list(range(1, ny - 1))
     across = [(x, x ^ 1) for x in range(nx) if x ^ 1 < nx]
     onward = [(x, x + 2) for x in range(0, nx - 2, 2)] + [(x, x - 2) for x in range(3, nx, 2)]
     whole = lambda route, rows: [(flat(a, y), flat(b, y)) for a, b in route for y in rows]
@@ -28,10 +27,10 @@
     return {
         "across": whole(across, range(ny)),
         "onward": whole(onward, range(ny)),
-        "across_edge": whole(across, middle),
-        "onward_edge": whole(onward, middle),
         "twins": [(flat(x, y), flat(x, y ^ 1)) for x in range(nx) for y in range(ny)],
         "seam": [(flat(x, a), flat(x, b)) for x in range(nx) for a, b in seams],
+        "seam_near": [(flat(x, a), flat(t, b)) for x, t in across for a, b in seams],
+        "seam_far": [(flat(x ^ 1, a), flat(t, b)) for x, t in onward for a, b in seams],
     }
 
 
@@ -151,6 +150,22 @@
     )(fields, *earlier)
 
 
+def gate_kernel(*refs):
+    pass
+
+
+def gate(block, *earlier):
+    return pl.pallas_call(
+        gate_kernel,
+        out_shape=jax.ShapeDtypeStruct(block.shape, F32),
+        in_specs=[HBM] * (1 + len(earlier)),
+        out_specs=HBM,
+        input_output_aliases={0: 0},
+        compiler_params=pltpu.CompilerParams(vmem_limit_bytes=SCOPED),
+        cost_estimate=pl.CostEstimate(flops=0, bytes_accessed=4096, transcendentals=0),
+    )(block, *earlier)
+
+
 def cut_kernel(many, plan, *rest):
     blocks, inner = rest[:many], rest[-1]
     cells, rows, _ = blocks[0].shape
@@ -301,17 +316,19 @@
     fields, inner, outer = gather(plan, source, receiver, count)
     own_twin = send(inner, "twins")
     own_edge = send(outer, "seam")
-    near.append(send(take(1, fields), "across"))
-    near_edge = send(own_edge, "across_edge")
-    far_edge = send(near_edge, "onward_edge")
+    near_edge = send(outer, "seam_near")
+    far_edge = send(outer, "seam_far")
+    near.append(send(take(1, fields, own_twin, own_edge, near_edge), "across"))
 
     far, twins, tokens = [], [], []
     outs = ()
     for s in range(count + 1):
         if s < count:
+            if s >= 2:
+                near[s] = gate(near[s], tokens[s - 2])
             far.append(send(near[s], "onward"))
             if s + 2 < count:
-                earlier = [near[s], own_twin, own_edge] if s == 0 else [near[s], far[s - 1], near_edge, twins[s - 1]]
+                earlier = [near[s], far_edge] if s == 0 else [near[s], far[s - 1], twins[s - 1]]
                 earlier = earlier + tokens[s - 2 : s - 1] if s >= 2 else earlier
                 near.append(send(take(s + 2, fields, *earlier), "across"))
         blocks = near[s : s + 1] + (far[s - 1 : s] if s >= 1 else [])

time: 158 us -> 136 us (0.86); the launches traced: 159 us -> 133 us
  waiting for transfers between devices: 74.7 us -> 54.1 us
  starting transfers between devices: 32.8 us -> 27.9 us
    ppermute x17, waiting for transfers between devices: 74.7 us -> 54.1 us  [work(): send = lambda value, route: lax.ppermute(value, ('gx', 'gy'), routes[route])]
    ppermute x17, starting transfers between devices: 32.8 us -> 27.9 us  [work(): send = lambda value, route: lax.ppermute(value, ('gx', 'gy'), routes[route])]
  transfers between devices with their start and end apart: 17 -> 17, of which waited for: 9 -> 9; matrix products, arithmetic and copies ran while one was open for 0% -> 0% of each run, Pallas kernels for 21% -> 26%
where the time goes in v1:
time: 136 us; the launch traced here: 133 us
  waiting for transfers between devices  54.1 us (40%)
  Pallas kernels  45.7 us (34%)
  starting transfers between devices  27.9 us (21%)
  local copies, waits for them, and re-layouts  4.1 us (3%)
    ppermute x17, waiting for transfers between devices, work(): send = lambda value, route: lax.ppermute(value, ('gx', 'gy'), routes[route])  54.1 us
    pallas_call x4, Pallas kernels, image(): pl.pallas_call(functools.partial(image_kernel, slot, spot), out_shape=[wh...  36.9 us
    ppermute x17, starting transfers between devices, work(): send = lambda value, route: lax.ppermute(value, ('gx', 'gy'), routes[route])  27.9 us
    pallas_call x5, Pallas kernels, cut(): pl.pallas_call(functools.partial(cut_kernel, len(blocks)), out_shape=jax....  3.57 us
  transfers between devices with their start and end apart: 17, of which 9 were waited for; matrix products, arithmetic and copies ran while one was open for 0% of the time, Pallas kernels for 26%

profile of v1, /device:TPU:7, one launch (start us, length us, event | category | flops | bytes accessed | tf_op | source)
XLA Modules:
  0.0 133.4 jit_solution(13298417675215743633)
XLA Ops:
  0.6 1.3 %copy.48.pairs = s32[3,2]{1,0:T(4,128)} copy(s32[3,2]{0,1:T(2,128)} %param.13) | data formatting | bytes 48 | tf_op args[2]
  2.0 1.6 %shard_map.77 = (s32[57]{0:T(128)S(1)}, f32[51]{0:T(128)S(1)}) custom-call(s32[3,2]{1,0:T(4,128)} %copy.48.pairs, s32[17]{0:T(128)} %lags.1, f32[4,17]{1,0:T(4,128)} %table.1, s32[3]{0:T(128)} %rows.1), custom_call_target="tpu_custom_call" | custom-call | tf_op jit(solution)/shard_map/pallas_call | solution.py:345
  3.6 0.6 slice.3
  4.8 128.6 %conditional.1 = (f32[3,48,16,256]{3,2,1,0:T(8,128)}, f32[3,48,16,256]{3,2,1,0:T(8,128)}) conditional(s32[]{:T(128)} %bitcast, (s32[57]{0:T(128)S(1)}, f32[4,48,16,256]{3,2,1,0:T(8,128)}, f32[4,48,16,256]{3,2,1,0:T(8,128)}, f32[51]{0:T(128)S(1)}) %tuple.27, (s32[57]{0:T(128)S(1)}, f32[4,48,16,256]{3,2,1,0:T(8,128)}, ...), branch_computations={%region_0.0_spmd, %region_1.0_spmd, %region_2.0_spmd, %region_3.0_... | conditional | flops 132000000 | bytes 250562096 | solution.py:357
  4.8 0.0 copy-start.12
  4.9 0.0 copy-start.17
  4.9 2.0 %branch_2_fun.18 = f32[48,16,256]{2,1,0:T(8,128)S(1)} custom-call(s32[57]{0:T(128)S(1)} %get-tuple-element.67.plan, f32[4,48,16,256]{3,2,1,0:T(8,128)} %get-tuple-element.69.source, f32[4,48,16,256]{3,2,1,0:T(8,128)} %get-tuple-element.70.receiver), custom_call_target="tpu_custom_call" | custom-call | bytes 1600000 | tf_op jit(solution)/shard_map/cond/branch_2_fun/pallas_call | solution.py:93
  6.8 1.4 %collective-permute-start.29 = (f32[48,16,256]{2,1,0:T(8,128)S(1)}, f32[48,16,256]{2,1,0:T(8,128)S(1)}, u32[]{:S(2)}, u32[]{:S(2)}) collective-permute-start(f32[48,16,256]{2,1,0:T(8,128)S(1)} %branch_2_fun.18), channel_id=1, source_target_pairs={{0,4},{1,5},{2,6},{3,7},{4,0},{5,1},{6,2},{7,3},{8,12},{9,13},{10,... | collective-permute-start | bytes 2359304 | tf_op jit(solution)/shard_map/cond/branch_2_fun/ppermute | solution.py:313
  8.2 0.0 copy-done.12
  8.2 0.0 copy-done.17
  8.2 1.5 %branch_2_fun.16 = (f32[4,48,16,256]{3,2,1,0:T(8,128)S(1)}, f32[4,48,2,256]{3,2,1,0:T(2,128)S(1)}, f32[4,48,2,256]{3,2,1,0:T(2,128)S(1)}) custom-call(s32[57]{0:T(128)S(1)} %get-tuple-element.67.plan, f32[4,48,16,256]{3,2,1,0:T(8,128)S(1)} %copy-done.12, f32[4,48,16,256]{3,2,1,0:T(8,128)S(1)} %copy-done.17), custom_call_target="tpu_custom_call" | custom-call | bytes 6000000 | tf_op jit(solution)/shard_map/cond/branch_2_fun/pallas_call | solution.py:123
  9.7 5.4 %collective-permute-start.26 = (f32[4,48,2,256]{3,2,1,0:T(2,128)S(1)}, f32[4,48,2,256]{3,2,1,0:T(2,128)S(1)}, u32[]{:S(2)}, u32[]{:S(2)}) collective-permute-start(f32[4,48,2,256]{3,2,1,0:T(2,128)S(1)} %get-tuple-element.73), channel_id=1, source_target_pairs={{1,2},{2,1},{5,6},{6,5},{9,10},{10,9},{13,14},{14,13},{17,18},{18,... | collective-permute-start | bytes 1179656 | tf_op jit(solution)/shard_map/cond/branch_2_fun/ppermute | solution.py:313
  15.1 2.1 %collective-permute-start.27 = (f32[4,48,2,256]{3,2,1,0:T(2,128)S(1)}, f32[4,48,2,256]{3,2,1,0:T(2,128)S(1)}, u32[]{:S(2)}, u32[]{:S(2)}) collective-permute-start(f32[4,48,2,256]{3,2,1,0:T(2,128)S(1)} %get-tuple-element.73), channel_id=1, source_target_pairs={{1,6},{2,5},{5,2},{6,1},{9,14},{10,13},{13,10},{14,9},{17,22},{18,... | collective-permute-start | bytes 1179656 | tf_op jit(solution)/shard_map/cond/branch_2_fun/ppermute | solution.py:313
  17.2 0.1 collective-permute-start.25
  17.3 21.2 %collective-permute-done.26.rest_1_.own_edge = f32[4,48,2,256]{3,2,1,0:T(2,128)S(1)} collective-permute-done((f32[4,48,2,256]{3,2,1,0:T(2,128)S(1)}, f32[4,48,2,256]{3,2,1,0:T(2,128)S(1)}, u32[]{:S(2)}, u32[]{:S(2)}) %collective-permute-start.26) | collective-permute-done | bytes 393248 | tf_op jit(solution)/shard_map/cond/branch_2_fun/ppermute | solution.py:313
  38.5 0.0 collective-permute-done.27.rest_2_.near_edge
  38.5 0.0 collective-permute-done.25.rest_0_.own_twin
  38.5 0.1 branch_2_fun.17
  38.6 0.1 collective-permute-start.28
  38.7 0.0 collective-permute-done.29.rest_0_.near
  38.7 3.3 %collective-permute-start.30 = (f32[48,16,256]{2,1,0:T(8,128)S(1)}, f32[48,16,256]{2,1,0:T(8,128)S(1)}, u32[]{:S(2)}, u32[]{:S(2)}) collective-permute-start(f32[48,16,256]{2,1,0:T(8,128)S(1)} %collective-permute-done.29.rest_0_.near), channel_id=1, source_target_pairs={{0,8},{1,9},{2,10},{3,11},{8,16},{9,17},{10,18},{11,19},{16,24},{1... | collective-permute-start | bytes 2359304 | tf_op jit(solution)/shard_map/cond/branch_2_fun/ppermute | solution.py:313
  42.0 4.8 %collective-permute-start.35 = (f32[4,48,2,256]{3,2,1,0:T(2,128)S(1)}, f32[4,48,2,256]{3,2,1,0:T(2,128)S(1)}, u32[]{:S(2)}, u32[]{:S(2)}) collective-permute-start(f32[4,48,2,256]{3,2,1,0:T(2,128)S(1)} %get-tuple-element.73), channel_id=1, source_target_pairs={{5,10},{6,9},{13,18},{14,17},{21,26},{22,25},{29,34},{30,33},{37,4... | collective-permute-start | bytes 1179656 | tf_op jit(solution)/shard_map/cond/branch_2_fun/ppermute | solution.py:313
  46.7 11.4 %collective-permute-done.35.rest_1_.far_edge = f32[4,48,2,256]{3,2,1,0:T(2,128)S(1)} collective-permute-done((f32[4,48,2,256]{3,2,1,0:T(2,128)S(1)}, f32[4,48,2,256]{3,2,1,0:T(2,128)S(1)}, u32[]{:S(2)}, u32[]{:S(2)}) %collective-permute-start.35) | collective-permute-done | bytes 393248 | tf_op jit(solution)/shard_map/cond/branch_2_fun/ppermute | solution.py:313
  58.1 0.1 branch_2_fun.22
  58.2 0.1 collective-permute-start.36
  58.3 0.0 collective-permute-done.28.rest_0_.near
  58.3 1.9 %collective-permute-start.33 = (f32[48,16,256]{2,1,0:T(8,128)S(1)}, f32[48,16,256]{2,1,0:T(8,128)S(1)}, u32[]{:S(2)}, u32[]{:S(2)}) collective-permute-start(f32[48,16,256]{2,1,0:T(8,128)S(1)} %collective-permute-done.28.rest_0_.near), channel_id=1, source_target_pairs={{0,8},{1,9},{2,10},{3,11},{8,16},{9,17},{10,18},{11,19},{16,24},{1... | collective-permute-start | bytes 2359304 | tf_op jit(solution)/shard_map/cond/branch_2_fun/ppermute | solution.py:313
  60.2 0.6 branch_2_fun.19
  60.9 0.1 collective-permute-start.31
  61.0 1.3 collective-permute-done.31.rest_2_.near_twin
  62.3 3.2 %collective-permute-done.30.rest_1_.far = f32[48,16,256]{2,1,0:T(8,128)S(1)} collective-permute-done((f32[48,16,256]{2,1,0:T(8,128)S(1)}, f32[48,16,256]{2,1,0:T(8,128)S(1)}, u32[]{:S(2)}, u32[]{:S(2)}) %collective-permute-start.30) | collective-permute-done | bytes 786464 | tf_op jit(solution)/shard_map/cond/branch_2_fun/ppermute | solution.py:313
  65.5 0.1 branch_2_fun.20
  65.6 0.3 collective-permute-start.32
  65.9 0.8 branch_2_fun.21
  66.7 0.4 collective-permute-start.34
  67.1 1.1 collective-permute-done.34.far_twin.near_twin
  68.2 11.5 %branch_2_fun.23 = (f32[3,48,16,256]{3,2,1,0:T(8,128)S(1)}, f32[3,48,16,256]{3,2,1,0:T(8,128)S(1)}, f32[8,128]{1,0:T(8,128)S(1)}) custom-call(s32[57]{0:T(128)S(1)} %get-tuple-element.67.plan, f32[51]{0:T(128)S(1)} %get-tuple-element.68.weights, f32[4,48,16,256]{3,2,1,0:T(8,128)S(1)} %get-tuple-element.71.fields, ...), custom_call_target="tpu_custom_call" | custom-call | flops 22000000 | bytes 22000000 | tf_op jit(solution)/shard_map/cond/branch_2_fun/pallas_call | solution.py:293
  79.7 0.0 collective-permute-done.36.refs_0_
  79.7 0.0 collective-permute-done.33.rest_1_.far
  79.7 0.8 branch_2_fun.25
  80.5 0.4 collective-permute-start.37
  80.9 2.0 %collective-permute-start.39 = (f32[48,16,256]{2,1,0:T(8,128)S(1)}, f32[48,16,256]{2,1,0:T(8,128)S(1)}, u32[]{:S(2)}, u32[]{:S(2)}) collective-permute-start(f32[48,16,256]{2,1,0:T(8,128)S(1)} %branch_2_fun.24.rest_0_.near), channel_id=1, source_target_pairs={{0,8},{1,9},{2,10},{3,11},{8,16},{9,17},{10,18},{11,19},{16,24},{1... | collective-permute-start | bytes 2359304 | tf_op jit(solution)/shard_map/cond/branch_2_fun/ppermute | solution.py:313
  82.9 0.0 collective-permute-done.37.far_twin.near_twin
  82.9 11.5 %branch_2_fun.26 = (f32[3,48,16,256]{3,2,1,0:T(8,128)S(1)}, f32[3,48,16,256]{3,2,1,0:T(8,128)S(1)}, f32[8,128]{1,0:T(8,128)S(1)}) custom-call(s32[57]{0:T(128)S(1)} %get-tuple-element.67.plan, f32[51]{0:T(128)S(1)} %get-tuple-element.68.weights, f32[4,48,16,256]{3,2,1,0:T(8,128)S(1)} %get-tuple-element.71.fields, ...), custom_call_target="tpu_custom_call", output_to_operand_aliasing={{0}: (11, {}), {1}: (12, {})} | custom-call | flops 22000000 | bytes 22000000 | tf_op jit(solution)/shard_map/cond/branch_2_fun/pallas_call | solution.py:293
  94.4 0.0 collective-permute-done.32.refs_0_
  94.4 3.2 %collective-permute-start.38 = (f32[48,16,256]{2,1,0:T(8,128)S(1)}, f32[48,16,256]{2,1,0:T(8,128)S(1)}, u32[]{:S(2)}, u32[]{:S(2)}) collective-permute-start(f32[48,16,256]{2,1,0:T(8,128)S(1)} %branch_2_fun.27.rest_0_.near), channel_id=1, source_target_pairs={{0,8},{1,9},{2,10},{3,11},{8,16},{9,17},{10,18},{11,19},{16,24},{1... | collective-permute-start | bytes 2359304 | tf_op jit(solution)/shard_map/cond/branch_2_fun/ppermute | solution.py:313
  97.6 6.9 %collective-permute-done.39.rest_1_.far = f32[48,16,256]{2,1,0:T(8,128)S(1)} collective-permute-done((f32[48,16,256]{2,1,0:T(8,128)S(1)}, f32[48,16,256]{2,1,0:T(8,128)S(1)}, u32[]{:S(2)}, u32[]{:S(2)}) %collective-permute-start.39) | collective-permute-done | bytes 786464 | tf_op jit(solution)/shard_map/cond/branch_2_fun/ppermute | solution.py:313
  104.5 0.8 branch_2_fun.28
  105.3 1.4 %collective-permute-start.40 = (f32[2,48,2,256]{3,2,1,0:T(2,128)S(1)}, f32[2,48,2,256]{3,2,1,0:T(2,128)S(1)}, u32[]{:S(2)}, u32[]{:S(2)}) collective-permute-start(f32[2,48,2,256]{3,2,1,0:T(2,128)S(1)} %branch_2_fun.28), channel_id=1, source_target_pairs={{0,1},{1,0},{2,3},{3,2},{4,5},{5,4},{6,7},{7,6},{8,9},{9,8},{10,11... | collective-permute-start | bytes 589832 | tf_op jit(solution)/shard_map/cond/branch_2_fun/ppermute | solution.py:313
  106.8 1.1 collective-permute-done.40.far_twin.near_twin
  107.8 6.7 %branch_2_fun.29 = (f32[3,48,16,256]{3,2,1,0:T(8,128)S(1)}, f32[3,48,16,256]{3,2,1,0:T(8,128)S(1)}, f32[8,128]{1,0:T(8,128)S(1)}) custom-call(s32[57]{0:T(128)S(1)} %get-tuple-element.67.plan, f32[51]{0:T(128)S(1)} %get-tuple-element.68.weights, f32[4,48,16,256]{3,2,1,0:T(8,128)S(1)} %get-tuple-element.71.fields, ...), custom_call_target="tpu_custom_call", output_to_operand_aliasing={{0}: (11, {}), {1}: (12, {})} | custom-call | flops 22000000 | bytes 22000000 | tf_op jit(solution)/shard_map/cond/branch_2_fun/pallas_call | solution.py:293
  114.5 6.9 %collective-permute-done.38.rest_0_.far = f32[48,16,256]{2,1,0:T(8,128)S(1)} collective-permute-done((f32[48,16,256]{2,1,0:T(8,128)S(1)}, f32[48,16,256]{2,1,0:T(8,128)S(1)}, u32[]{:S(2)}, u32[]{:S(2)}) %collective-permute-start.38) | collective-permute-done | bytes 786464 | tf_op jit(solution)/shard_map/cond/branch_2_fun/ppermute | solution.py:313
  121.4 0.6 branch_2_fun.30
  122.1 1.0 collective-permute-start.41
  123.0 0.9 collective-permute-done.41.far_twin
  124.0 7.2 %branch_2_fun.31 = (f32[3,48,16,256]{3,2,1,0:T(8,128)S(1)}, f32[3,48,16,256]{3,2,1,0:T(8,128)S(1)}, f32[8,128]{1,0:T(8,128)}) custom-call(s32[57]{0:T(128)S(1)} %get-tuple-element.67.plan, f32[51]{0:T(128)S(1)} %get-tuple-element.68.weights, f32[4,48,16,256]{3,2,1,0:T(8,128)S(1)} %get-tuple-element.71.fields, ...), custom_call_target="tpu_custom_call", output_to_operand_aliasing={{0}: (11, {}), {1}: (12, {})} | custom-call | flops 22000000 | bytes 22000000 | tf_op jit(solution)/shard_map/cond/branch_2_fun/pallas_call | solution.py:293
  131.2 0.0 copy-start.2
  131.2 0.0 copy-start.7
  131.2 1.4 %copy-done.2 = f32[3,48,16,256]{3,2,1,0:T(8,128)} copy-done((f32[3,48,16,256]{3,2,1,0:T(8,128)}, f32[3,48,16,256]{3,2,1,0:T(8,128)S(1)}, u32[]{:S(2)}) %copy-start.2) | copy-done | bytes 2359320 | tf_op jit(solution)/shard_map/cond
  132.6 0.8 copy-done.7
  (2 shorter events, 0.0 us)
Async XLA Ops:
  4.8 3.4 %copy-start.12 = (f32[4,48,16,256]{3,2,1,0:T(8,128)S(1)}, f32[4,48,16,256]{3,2,1,0:T(8,128)}, u32[]{:S(2)}) copy-start(f32[4,48,16,256]{3,2,1,0:T(8,128)} %get-tuple-element.69.source) | copy-start | bytes 9437188 | tf_op jit(solution)/shard_map/cond
  4.9 3.4 %copy-start.17 = (f32[4,48,16,256]{3,2,1,0:T(8,128)S(1)}, f32[4,48,16,256]{3,2,1,0:T(8,128)}, u32[]{:S(2)}) copy-start(f32[4,48,16,256]{3,2,1,0:T(8,128)} %get-tuple-element.70.receiver) | copy-start | bytes 9437188 | tf_op jit(solution)/shard_map/cond
  6.8 31.8 %collective-permute-start.29 = (f32[48,16,256]{2,1,0:T(8,128)S(1)}, f32[48,16,256]{2,1,0:T(8,128)S(1)}, u32[]{:S(2)}, u32[]{:S(2)}) collective-permute-start(f32[48,16,256]{2,1,0:T(8,128)S(1)} %branch_2_fun.18), channel_id=1, source_target_pairs={{0,4},{1,5},{2,6},{3,7},{4,0},{5,1},{6,2},{7,3},{8,12},{9,13},{10,... | collective-permute-start | bytes 2359304 | tf_op jit(solution)/shard_map/cond/branch_2_fun/ppermute | solution.py:313
  9.7 28.8 %collective-permute-start.26 = (f32[4,48,2,256]{3,2,1,0:T(2,128)S(1)}, f32[4,48,2,256]{3,2,1,0:T(2,128)S(1)}, u32[]{:S(2)}, u32[]{:S(2)}) collective-permute-start(f32[4,48,2,256]{3,2,1,0:T(2,128)S(1)} %get-tuple-element.73), channel_id=1, source_target_pairs={{1,2},{2,1},{5,6},{6,5},{9,10},{10,9},{13,14},{14,13},{17,18},{18,... | collective-permute-start | bytes 1179656 | tf_op jit(solution)/shard_map/cond/branch_2_fun/ppermute | solution.py:313
  15.1 23.4 %collective-permute-start.27 = (f32[4,48,2,256]{3,2,1,0:T(2,128)S(1)}, f32[4,48,2,256]{3,2,1,0:T(2,128)S(1)}, u32[]{:S(2)}, u32[]{:S(2)}) collective-permute-start(f32[4,48,2,256]{3,2,1,0:T(2,128)S(1)} %get-tuple-element.73), channel_id=1, source_target_pairs={{1,6},{2,5},{5,2},{6,1},{9,14},{10,13},{13,10},{14,9},{17,22},{18,... | collective-permute-start | bytes 1179656 | tf_op jit(solution)/shard_map/cond/branch_2_fun/ppermute | solution.py:313
  17.2 21.3 %collective-permute-start.25 = (f32[4,48,2,256]{3,2,1,0:T(2,128)S(1)}, f32[4,48,2,256]{3,2,1,0:T(2,128)S(1)}, u32[]{:S(2)}, u32[]{:S(2)}) collective-permute-start(f32[4,48,2,256]{3,2,1,0:T(2,128)S(1)} %get-tuple-element.72), channel_id=1, source_target_pairs={{0,1},{1,0},{2,3},{3,2},{4,5},{5,4},{6,7},{7,6},{8,9},{9,8},{10,11... | collective-permute-start | bytes 1179656 | tf_op jit(solution)/shard_map/cond/branch_2_fun/ppermute | solution.py:313
  38.6 19.7 %collective-permute-start.28 = (f32[48,16,256]{2,1,0:T(8,128)S(1)}, f32[48,16,256]{2,1,0:T(8,128)S(1)}, u32[]{:S(2)}, u32[]{:S(2)}) collective-permute-start(f32[48,16,256]{2,1,0:T(8,128)S(1)} %branch_2_fun.17), channel_id=1, source_target_pairs={{0,4},{1,5},{2,6},{3,7},{4,0},{5,1},{6,2},{7,3},{8,12},{9,13},{10,... | collective-permute-start | bytes 2359304 | tf_op jit(solution)/shard_map/cond/branch_2_fun/ppermute | solution.py:313
  38.7 26.8 %collective-permute-start.30 = (f32[48,16,256]{2,1,0:T(8,128)S(1)}, f32[48,16,256]{2,1,0:T(8,128)S(1)}, u32[]{:S(2)}, u32[]{:S(2)}) collective-permute-start(f32[48,16,256]{2,1,0:T(8,128)S(1)} %collective-permute-done.29.rest_0_.near), channel_id=1, source_target_pairs={{0,8},{1,9},{2,10},{3,11},{8,16},{9,17},{10,18},{11,19},{16,24},{1... | collective-permute-start | bytes 2359304 | tf_op jit(solution)/shard_map/cond/branch_2_fun/ppermute | solution.py:313
  42.0 16.2 %collective-permute-start.35 = (f32[4,48,2,256]{3,2,1,0:T(2,128)S(1)}, f32[4,48,2,256]{3,2,1,0:T(2,128)S(1)}, u32[]{:S(2)}, u32[]{:S(2)}) collective-permute-start(f32[4,48,2,256]{3,2,1,0:T(2,128)S(1)} %get-tuple-element.73), channel_id=1, source_target_pairs={{5,10},{6,9},{13,18},{14,17},{21,26},{22,25},{29,34},{30,33},{37,4... | collective-permute-start | bytes 1179656 | tf_op jit(solution)/shard_map/cond/branch_2_fun/ppermute | solution.py:313
  58.2 21.5 %collective-permute-start.36 = (f32[48,16,256]{2,1,0:T(8,128)S(1)}, f32[48,16,256]{2,1,0:T(8,128)S(1)}, u32[]{:S(2)}, u32[]{:S(2)}) collective-permute-start(f32[48,16,256]{2,1,0:T(8,128)S(1)} %branch_2_fun.22), channel_id=1, source_target_pairs={{0,4},{1,5},{2,6},{3,7},{4,0},{5,1},{6,2},{7,3},{8,12},{9,13},{10,... | collective-permute-start | bytes 2359304 | tf_op jit(solution)/shard_map/cond/branch_2_fun/ppermute | solution.py:313
  58.3 21.4 %collective-permute-start.33 = (f32[48,16,256]{2,1,0:T(8,128)S(1)}, f32[48,16,256]{2,1,0:T(8,128)S(1)}, u32[]{:S(2)}, u32[]{:S(2)}) collective-permute-start(f32[48,16,256]{2,1,0:T(8,128)S(1)} %collective-permute-done.28.rest_0_.near), channel_id=1, source_target_pairs={{0,8},{1,9},{2,10},{3,11},{8,16},{9,17},{10,18},{11,19},{16,24},{1... | collective-permute-start | bytes 2359304 | tf_op jit(solution)/shard_map/cond/branch_2_fun/ppermute | solution.py:313
  60.9 1.4 %collective-permute-start.31 = (f32[1,48,2,256]{3,2,1,0:T(2,128)S(1)}, f32[1,48,2,256]{3,2,1,0:T(2,128)S(1)}, u32[]{:S(2)}, u32[]{:S(2)}) collective-permute-start(f32[1,48,2,256]{3,2,1,0:T(2,128)S(1)} %branch_2_fun.19), channel_id=1, source_target_pairs={{0,1},{1,0},{2,3},{3,2},{4,5},{5,4},{6,7},{7,6},{8,9},{9,8},{10,11... | collective-permute-start | bytes 294920 | tf_op jit(solution)/shard_map/cond/branch_2_fun/ppermute | solution.py:313
  65.6 28.9 %collective-permute-start.32 = (f32[48,16,256]{2,1,0:T(8,128)S(1)}, f32[48,16,256]{2,1,0:T(8,128)S(1)}, u32[]{:S(2)}, u32[]{:S(2)}) collective-permute-start(f32[48,16,256]{2,1,0:T(8,128)S(1)} %branch_2_fun.20), channel_id=1, source_target_pairs={{0,4},{1,5},{2,6},{3,7},{4,0},{5,1},{6,2},{7,3},{8,12},{9,13},{10,... | collective-permute-start | bytes 2359304 | tf_op jit(solution)/shard_map/cond/branch_2_fun/ppermute | solution.py:313
  66.7 1.5 %collective-permute-start.34 = (f32[2,48,2,256]{3,2,1,0:T(2,128)S(1)}, f32[2,48,2,256]{3,2,1,0:T(2,128)S(1)}, u32[]{:S(2)}, u32[]{:S(2)}) collective-permute-start(f32[2,48,2,256]{3,2,1,0:T(2,128)S(1)} %branch_2_fun.21), channel_id=1, source_target_pairs={{0,1},{1,0},{2,3},{3,2},{4,5},{5,4},{6,7},{7,6},{8,9},{9,8},{10,11... | collective-permute-start | bytes 589832 | tf_op jit(solution)/shard_map/cond/branch_2_fun/ppermute | solution.py:313
  80.5 2.4 %collective-permute-start.37 = (f32[2,48,2,256]{3,2,1,0:T(2,128)S(1)}, f32[2,48,2,256]{3,2,1,0:T(2,128)S(1)}, u32[]{:S(2)}, u32[]{:S(2)}) collective-permute-start(f32[2,48,2,256]{3,2,1,0:T(2,128)S(1)} %branch_2_fun.25), channel_id=1, source_target_pairs={{0,1},{1,0},{2,3},{3,2},{4,5},{5,4},{6,7},{7,6},{8,9},{9,8},{10,11... | collective-permute-start | bytes 589832 | tf_op jit(solution)/shard_map/cond/branch_2_fun/ppermute | solution.py:313
  80.9 23.6 %collective-permute-start.39 = (f32[48,16,256]{2,1,0:T(8,128)S(1)}, f32[48,16,256]{2,1,0:T(8,128)S(1)}, u32[]{:S(2)}, u32[]{:S(2)}) collective-permute-start(f32[48,16,256]{2,1,0:T(8,128)S(1)} %branch_2_fun.24.rest_0_.near), channel_id=1, source_target_pairs={{0,8},{1,9},{2,10},{3,11},{8,16},{9,17},{10,18},{11,19},{16,24},{1... | collective-permute-start | bytes 2359304 | tf_op jit(solution)/shard_map/cond/branch_2_fun/ppermute | solution.py:313
  94.4 26.9 %collective-permute-start.38 = (f32[48,16,256]{2,1,0:T(8,128)S(1)}, f32[48,16,256]{2,1,0:T(8,128)S(1)}, u32[]{:S(2)}, u32[]{:S(2)}) collective-permute-start(f32[48,16,256]{2,1,0:T(8,128)S(1)} %branch_2_fun.27.rest_0_.near), channel_id=1, source_target_pairs={{0,8},{1,9},{2,10},{3,11},{8,16},{9,17},{10,18},{11,19},{16,24},{1... | collective-permute-start | bytes 2359304 | tf_op jit(solution)/shard_map/cond/branch_2_fun/ppermute | solution.py:313
  105.3 2.5 %collective-permute-start.40 = (f32[2,48,2,256]{3,2,1,0:T(2,128)S(1)}, f32[2,48,2,256]{3,2,1,0:T(2,128)S(1)}, u32[]{:S(2)}, u32[]{:S(2)}) collective-permute-start(f32[2,48,2,256]{3,2,1,0:T(2,128)S(1)} %branch_2_fun.28), channel_id=1, source_target_pairs={{0,1},{1,0},{2,3},{3,2},{4,5},{5,4},{6,7},{7,6},{8,9},{9,8},{10,11... | collective-permute-start | bytes 589832 | tf_op jit(solution)/shard_map/cond/branch_2_fun/ppermute | solution.py:313
  122.1 1.9 %collective-permute-start.41 = (f32[1,48,2,256]{3,2,1,0:T(2,128)S(1)}, f32[1,48,2,256]{3,2,1,0:T(2,128)S(1)}, u32[]{:S(2)}, u32[]{:S(2)}) collective-permute-start(f32[1,48,2,256]{3,2,1,0:T(2,128)S(1)} %branch_2_fun.30), channel_id=1, source_target_pairs={{0,1},{1,0},{2,3},{3,2},{4,5},{5,4},{6,7},{7,6},{8,9},{9,8},{10,11... | collective-permute-start | bytes 294920 | tf_op jit(solution)/shard_map/cond/branch_2_fun/ppermute | solution.py:313
  131.2 1.4 %copy-start.2 = (f32[3,48,16,256]{3,2,1,0:T(8,128)}, f32[3,48,16,256]{3,2,1,0:T(8,128)S(1)}, u32[]{:S(2)}) copy-start(f32[3,48,16,256]{3,2,1,0:T(8,128)S(1)} %get-tuple-element.140) | copy-start | bytes 7077892 | tf_op jit(solution)/shard_map/cond
  131.2 2.2 %copy-start.7 = (f32[3,48,16,256]{3,2,1,0:T(8,128)}, f32[3,48,16,256]{3,2,1,0:T(8,128)S(1)}, u32[]{:S(2)}) copy-start(f32[3,48,16,256]{3,2,1,0:T(8,128)S(1)} %get-tuple-element.141) | copy-start | bytes 7077892 | tf_op jit(solution)/shard_map/cond

commit v2 on v0

v2 whole, which is shorter than its diff:
```python
import functools

import jax
import jax.numpy as jnp
from jax import lax
from jax.experimental import pallas as pl
from jax.experimental.pallas import tpu as pltpu
from jax.sharding import PartitionSpec as P

F32 = jnp.float32
SMEM = pl.BlockSpec(memory_space=pltpu.SMEM)
VMEM = pl.BlockSpec(memory_space=pltpu.VMEM)
HBM = pl.BlockSpec(memory_space=pl.ANY)
SCOPED = 24 * 2**20

ODD, SECOND, COUNT, FIELD, SLOT, FIRST, ORDER, LAG = 0, 1, 2, 8, 16, 24, 32, 40


def moves(mesh):
    nx, ny = mesh.shape["gx"], mesh.shape["gy"]
    flat = lambda x, y: x * ny + y
    across = [(x, x ^ 1) for x in range(nx) if x ^ 1 < nx]
    onward = [(x, x + 2) for x in range(0, nx - 2, 2)] + [(x, x - 2) for x in range(3, nx, 2)]
    whole = lambda route, rows: [(flat(a, y), flat(b, y)) for a, b in route for y in rows]
    seams = [(a, b) for y in range(1, ny - 1, 2) for a, b in ((y, y + 1), (y + 1, y))]
    return {
        "across": whole(across, range(ny)),
        "onward": whole(onward, range(ny)),
        "twins": [(flat(x, y), flat(x, y ^ 1)) for x in range(nx) for y in range(ny)],
        "seam": [(flat(x, a), flat(x, b)) for x in range(nx) for a, b in seams],
        "seam_near": [(flat(x, a), flat(t, b)) for x, t in across for a, b in seams],
        "seam_far": [(flat(x ^ 1, a), flat(t, b)) for x, t in onward for a, b in seams],
    }


def plan_kernel(snaps, pairs, lags, table, rows, plan, weights):
    units = 2 * pairs.shape[0]
    plan[ODD] = lax.rem(lax.axis_index("gx"), 2)
    plan[SECOND] = lax.rem(lax.axis_index("gy"), 2)
    ids = [pairs[u // 2, 1] if u % 2 == 0 else pairs[u // 2, 0] + snaps for u in range(units)]
    same = [[(ids[u] == ids[v]).astype(jnp.int32) for v in range(units)] for u in range(units)]
    uses = [sum(same[u]) for u in range(units)]
    leads = [jnp.int32(1)]
    for u in range(1, units):
        leads.append((sum(same[u][:u]) == 0).astype(jnp.int32))
    rank = []
    for u in range(units):
        ahead = jnp.int32(0)
        for v in range(units):
            if v != u:
                sooner = uses[v] >= uses[u] if v < u else uses[v] > uses[u]
                ahead = ahead + leads[v] * sooner.astype(jnp.int32)
        rank.append(ahead)
    slots = [sum(same[u][v] * leads[v] * rank[v] for v in range(units)) for u in range(units)]
    plan[COUNT] = sum(leads)
    for u in range(units):
        plan[SLOT + u] = slots[u]
        plan[FIELD + slots[u]] = ids[u]
        before = jnp.int32(0)
        for v in range(units):
            if v != u:
                sooner = slots[v] <= slots[u] if v < u else slots[v] < slots[u]
                before = before + sooner.astype(jnp.int32)
        plan[ORDER + before] = u
        plan[FIRST + u] = sum((slots[v] < u).astype(jnp.int32) for v in range(units))
    plan[FIRST + units] = units
    for h in range(lags.shape[0]):
        plan[LAG + h] = 2 * lags[h]
        for p in range(pairs.shape[0]):
            weights[p * lags.shape[0] + h] = table[rows[p], h]


def launch(kernel, inputs, outputs, scratch, earlier, aliases=None):
    begin, end = len(inputs), len(inputs) + len(earlier)

    def body(*refs):
        results = refs[end : end + len(outputs)]
        token = refs[end + len(outputs)]
        kernel(*refs[:begin], *results, *refs[end + len(outputs) + 1 :])
        token[...] = jnp.zeros_like(token)

    return pl.pallas_call(
        body,
        out_shape=[shape for shape, _ in outputs] + [jax.ShapeDtypeStruct((8, 128), F32)],
        in_specs=[memory for _, memory in inputs] + [HBM] * len(earlier),
        out_specs=[memory for _, memory in outputs] + [VMEM],
        scratch_shapes=scratch,
        input_output_aliases=aliases or {},
        compiler_params=pltpu.CompilerParams(vmem_limit_bytes=SCOPED),
        cost_estimate=pl.CostEstimate(flops=0, bytes_accessed=2000000, transcendentals=0),
    )(*[array for array, _ in inputs], *earlier)


def fetch(field, source, receiver, target, sem):
    snaps = receiver.shape[0]
    width = pl.ds(0, target.shape[-1])

    @pl.when(field < snaps)
    def _():
        pltpu.make_async_copy(receiver.at[jnp.minimum(field, snaps - 1), :, :, width], target, sem).start()

    @pl.when(field >= snaps)
    def _():
        pltpu.make_async_copy(source.at[jnp.maximum(field - snaps, 0), :, :, width], target, sem).start()

    return pltpu.make_async_copy(receiver.at[0, :, :, width], target, sem)


def lead_kernel(plan, source, receiver, out, sem):
    fetch(plan[FIELD], source, receiver, out, sem).wait()


def lead(plan, source, receiver, width):
    block = jax.ShapeDtypeStruct(source.shape[1:3] + (width,), F32)
    inputs = [(plan, SMEM), (source, HBM), (receiver, HBM)]
    return launch(lead_kernel, inputs, [(block, VMEM)], [pltpu.SemaphoreType.DMA], [])


def gather_kernel(plan, source, receiver, fields, inner, outer, sems):
    count, cells, rows, _ = fields.shape
    waits = [fetch(plan[FIELD + s], source, receiver, fields.at[s], sems.at[s]) for s in range(count)]
    second = plan[SECOND] == 1
    for s, wait in enumerate(waits):
        wait.wait()

        def rim(x, carry):
            low, high = fields[s, x, 0:2], fields[s, x, rows - 2 : rows]
            inner[s, x] = jnp.where(second, low, high)
            outer[s, x] = jnp.where(second, high, low)
            return carry

        lax.fori_loop(0, cells, rim, 0, unroll=4)


def gather(plan, source, receiver, count, earlier):
    _, cells, rows, depth = source.shape
    edge = jax.ShapeDtypeStruct((count, cells, 2, depth), F32)
    whole = jax.ShapeDtypeStruct((count, cells, rows, depth), F32)
    inputs = [(plan, SMEM), (source, HBM), (receiver, HBM)]
    outputs = [(whole, VMEM), (edge, VMEM), (edge, VMEM)]
    return launch(gather_kernel, inputs, outputs, [pltpu.SemaphoreType.DMA((count,))], earlier)


def take_kernel(piece, fields, out, sem):
    slot, start, width = piece
    copy = pltpu.make_async_copy(fields.at[slot, :, :, pl.ds(start, width)], out, sem)
    copy.start()
    copy.wait()


def take(piece, fields, earlier):
    block = jax.ShapeDtypeStruct(fields.shape[1:3] + piece[2:], F32)
    kernel = functools.partial(take_kernel, piece)
    return launch(kernel, [(fields, HBM)], [(block, VMEM)], [pltpu.SemaphoreType.DMA], earlier)


def turn_kernel(piece, block, fields, same, out, sem):
    take_kernel(piece, fields, out, sem)


def turn(block, piece, fields, earlier):
    shape = jax.ShapeDtypeStruct(block.shape, F32)
    out = jax.ShapeDtypeStruct(fields.shape[1:3] + piece[2:], F32)
    kernel = functools.partial(turn_kernel, piece)
    outputs = [(shape, HBM), (out, VMEM)]
    return launch(kernel, [(block, HBM), (fields, HBM)], outputs, [pltpu.SemaphoreType.DMA], earlier, {0: 0})


def gate_kernel(block, same):
    pass


def gate(block, earlier):
    shape = jax.ShapeDtypeStruct(block.shape, F32)
    return launch(gate_kernel, [(block, HBM)], [(shape, HBM)], [], earlier, {0: 0})


def cut_kernel(many, plan, *rest):
    blocks, inner = rest[:many], rest[many]
    cells, rows, _ = blocks[0].shape
    second = plan[SECOND] == 1
    start = 0
    for block in blocks:
        lanes = slice(start, start + block.shape[2])
        start = lanes.stop

        def rim(x, carry):
            inner[x, :, lanes] = jnp.where(second, block[x, 0:2], block[x, rows - 2 : rows])
            return carry

        lax.fori_loop(0, cells, rim, 0, unroll=4)


def cut_type(blocks):
    return jax.ShapeDtypeStruct((blocks[0].shape[0], 2, sum(block.shape[2] for block in blocks)), F32)


def cut(plan, blocks, earlier):
    inputs = [(plan, SMEM)] + [(block, VMEM) for block in blocks]
    return launch(functools.partial(cut_kernel, len(blocks)), inputs, [(cut_type(blocks), VMEM)], [], earlier)


def image_kernel(
    piece, spot, plan, weights, fields, near, far, own_twin, own_edge, near_twin, near_edge, far_twin, far_edge, *rest
):
    to_source, to_receiver, ext, prod, mix, mext, done, sems = rest[-8:]
    slot, start, _ = piece
    _, cells, rows, _ = fields.shape
    halves, lanes = ext.shape[0], ext.shape[3]
    pairs = to_source.shape[0]
    taps = weights.shape[0] // pairs
    odd, second = plan[ODD], plan[SECOND] == 1
    near_at = jnp.where(odd == 1, 0, 2 * cells)
    far_at = 2 * cells - near_at
    first, last = plan[FIRST + slot], plan[FIRST + slot + 1]
    part = [slice(z * lanes, (z + 1) * lanes) for z in range(halves)]
    whole = [slice(start + z * lanes, start + (z + 1) * lanes) for z in range(halves)]
    passed = [slice(spot + z * lanes, spot + (z + 1) * lanes) for z in range(halves)]
    low_tile = lax.broadcasted_iota(jnp.int32, (8, lanes), 0)

    def widen(target, at, block, block_lanes, twin, twin_lanes, edge):
        def one(x, carry):
            for z in range(halves):
                t, e = twin[x, :, twin_lanes[z]], edge[x, :, whole[z]]
                target[z, at + x, 8 : rows + 8] = block[x, :, block_lanes[z]]
                target[z, at + x, 6:8] = jnp.where(second, t, e)
                target[z, at + x, rows + 8 : rows + 10] = jnp.where(second, e, t)
            return carry

        lax.fori_loop(0, cells, one, 0, unroll=4)

    widen(ext, cells, fields.at[slot], whole, own_twin.at[slot], whole, own_edge.at[slot])
    widen(ext, near_at, near, part, near_twin, part, near_edge.at[slot])
    widen(ext, far_at, far, part, far_twin, passed, far_edge.at[slot])

    def product(x, carry):
        for z in range(halves):
            e, q = ext.at[z, x], prod.at[z, x]
            here = e[8 : rows + 8]
            q[0:rows] = here * here
            q[rows : 2 * rows] = here * e[9 : rows + 9]
            q[2 * rows : 3 * rows] = here * e[10 : rows + 10]
            base = e[0:8]
            one = base * e[1:9]
            two = base * e[2:10]
            q[3 * rows : 3 * rows + 8] = jnp.where(low_tile >= 6, two, pltpu.roll(one, 6, 0))
        return carry

    lax.fori_loop(0, 3 * cells, product, 0, unroll=4)

    def window(target, p):
        return target.at[p, :, :, pl.ds(start, halves * lanes)]

    def unit(index, carry):
        i = index - first
        u = plan[ORDER + index]
        to_r = lax.rem(u, 2)
        p = lax.div(u, 2)
        mate = plan[SLOT + u + 1 - 2 * to_r]
        sign = 1 - 2 * to_r
        at = [cells + sign * plan[LAG + h] for h in range(taps)]
        scale = [weights[p * taps + h] for h in range(taps)]
        widen(mext, 0, fields.at[mate], whole, own_twin.at[mate], whole, own_edge.at[mate])

        def total(x, carry):
            for z in range(halves):
                m, s = mix.at[z], mext.at[z, x]
                acc = None
                for h in range(taps):
                    term = scale[h] * prod[z, x + at[h]]
                    acc = term if acc is None else acc + term
                m[0, 8 : rows + 8] = acc[rows : 2 * rows]
                m[1, 8 : rows + 8] = acc[2 * rows : 3 * rows]
                extra = acc[3 * rows : 3 * rows + 8]
                m[0, 0:8] = pltpu.roll(extra, 2, 0)
                m[1, 0:8] = extra
                one = acc[rows : 2 * rows] * s[9 : rows + 9] + m[0, 7 : rows + 7] * s[7 : rows + 7]
                two = acc[2 * rows : 3 * rows] * s[10 : rows + 10] + m[1, 6 : rows + 6] * s[6 : rows + 6]
                done[i, x, :, part[z]] = 0.375 * (acc[0:rows] * s[8 : rows + 8]) + 0.25 * one + 0.0625 * two
            return carry

        lax.fori_loop(0, cells, total, 0)
        for which, target in enumerate((to_source, to_receiver)):

            @pl.when(to_r == which)
            def _():
                pltpu.make_async_copy(done.at[i], window(target, p), sems.at[i]).start()

        return carry

    lax.fori_loop(first, last, unit, 0)

    def settle(index, carry):
        i = index - first
        pltpu.make_async_copy(done.at[i], window(to_source, 0), sems.at[i]).wait()
        return carry

    lax.fori_loop(first, last, settle, 0)


def joint_kernel(many, piece, spot, news, *refs):
    plan, blocks, begin = refs[0], refs[1 : 1 + many], 1 + many
    results = refs[begin + 10 + news :]
    if many:
        cut_kernel(many, plan, *blocks, results[0])
        results = results[1:]
    image_kernel(piece, spot, plan, *refs[begin : begin + 10], *results)


def image(blocks, piece, pairs, plan, weights, fields, near, far, halos, spot, outs, earlier):
    _, cells, rows, depth = fields.shape
    whole = jax.ShapeDtypeStruct((pairs, cells, rows, depth), F32)
    lanes = 128 if piece[2] % 128 == 0 else piece[2]
    halves = piece[2] // lanes
    inputs = [(plan, SMEM)] + [(block, VMEM) for block in blocks]
    inputs += [(weights, SMEM), (fields, VMEM), (near, VMEM), (far, VMEM)] + [(halo, VMEM) for halo in halos]
    first = len(inputs)
    inputs += [(out, HBM) for out in outs]
    outputs = ([(cut_type(blocks), VMEM)] if blocks else []) + [(whole, HBM), (whole, HBM)]
    scratch = [
        pltpu.VMEM((halves, 3 * cells, rows + 16, lanes), F32),
        pltpu.VMEM((halves, 3 * cells, 3 * rows + 8, lanes), F32),
        pltpu.VMEM((halves, 2, rows + 8, lanes), F32),
        pltpu.VMEM((halves, cells, rows + 16, lanes), F32),
        pltpu.VMEM((pairs, cells, rows, halves * lanes), F32),
        pltpu.SemaphoreType.DMA((pairs,)),
    ]
    kernel = functools.partial(joint_kernel, len(blocks), piece, spot, len(outs))
    aliases = {first + i: len(outputs) - 2 + i for i in range(len(outs))}
    return launch(kernel, inputs, outputs, scratch, earlier, aliases)


AHEAD, TWINS = 2, 1
SPLIT_FIRST, SPLIT_LAST = False, False


def pieces_of(count, depth):
    pieces = []
    for slot in range(count):
        halved = depth % 256 == 0 and ((SPLIT_LAST and slot == count - 1) or (SPLIT_FIRST and slot == 0))
        width = depth // 2 if halved else depth
        pieces += [(slot, start, width) for start in range(0, depth, width)]
    return pieces


def work(count, pairs, routes, plan, weights, source, receiver):
    send = lambda value, route: lax.ppermute(value, ("gx", "gy"), routes[route])
    pieces = pieces_of(count, source.shape[3])
    last = len(pieces)

    first, token = lead(plan, source, receiver, pieces[0][2])
    near = [send(first, "across")]
    fields, inner, outer, token = gather(plan, source, receiver, count, [token])
    own_edge = send(outer, "seam")
    near_edge = send(outer, "seam_near")
    far_edge = send(outer, "seam_far")
    own_twin = send(inner, "twins")
    earlier = [own_twin, own_edge, near_edge]
    for piece in pieces[1:AHEAD]:
        block, token = take(piece, fields, [token] + earlier)
        near.append(send(block, "across"))
        earlier = []

    far, twins, outs = [], [], ()

    def sums(blocks, k, outs, token):
        halos = (own_twin, own_edge, twins[k], near_edge, twins[k + 1], far_edge)
        spot = pieces[k + 1][2] if k + 1 < last else 0
        *edge, to_source, to_receiver, token = image(
            blocks, pieces[k], pairs, plan, weights, fields, near[k], far[k], halos, spot, outs, [token]
        )
        return edge, (to_source, to_receiver), token

    for k in range(last):
        earlier = [token] + ([far_edge] if k == 0 else twins[k - TWINS : k - TWINS + 1] if TWINS <= k else [])
        if k + AHEAD < last:
            near[k], block, token = turn(near[k], pieces[k + AHEAD], fields, earlier)
            near.append(send(block, "across"))
        else:
            near[k], token = gate(near[k], earlier)
        far.append(send(near[k], "onward"))
        blocks = near[k : k + 1] + (far[k - 1 : k] if k >= 1 else [])
        if k < 2:
            edge, token = cut(plan, blocks, [token])
        else:
            (edge,), outs, token = sums(blocks, k - 2, outs, token)
        twins.append(send(edge, "twins"))
    _, outs, token = sums([], last - 2, outs, token)
    edge, token = cut(plan, far[last - 1 :], [token])
    twins.append(send(edge, "twins"))
    _, outs, token = sums([], last - 1, outs, token)
    return outs


def local(routes, source_snaps, receiver_snaps, snap_pairs, offset_lags, weight_table, weight_index):
    pairs = snap_pairs.shape[0]
    plan, weights = pl.pallas_call(
        functools.partial(plan_kernel, receiver_snaps.shape[0]),
        out_shape=[
            jax.ShapeDtypeStruct((LAG + offset_lags.shape[0],), jnp.int32),
            jax.ShapeDtypeStruct((pairs * offset_lags.shape[0],), F32),
        ],
        in_specs=[SMEM] * 4,
        out_specs=[SMEM] * 2,
    )(snap_pairs, offset_lags, weight_table, weight_index)
    least = 2
    most = 2 * pairs
    branches = [functools.partial(work, count, pairs, routes) for count in range(least, most + 1)]
    return lax.switch(plan[COUNT] - least, branches, plan, weights, source_snaps, receiver_snaps)


def solution(mesh):
    routes = moves(mesh)
    split = P(None, "gx", "gy", None)
    return jax.shard_map(
        functools.partial(local, routes),
        mesh=mesh,
        in_specs=(split, split, P(), P(), P(), P()),
        out_specs=(split, split),
        check_vma=False,
    )
```

time: 158 us -> 143 us (0.905); the launches traced: 159 us -> 140 us
  waiting for transfers between devices: 74.7 us -> 39.2 us
  starting transfers between devices: 32.8 us -> 48.9 us
    ppermute x17 -> x20, waiting for transfers between devices: 74.7 us -> 39.2 us  [work(): send = lambda value, route: lax.ppermute(value, ('gx', 'gy'), routes[route])]
    ppermute x17 -> x20, starting transfers between devices: 32.8 us -> 48.9 us  [work(): send = lambda value, route: lax.ppermute(value, ('gx', 'gy'), routes[route])]
    pallas_call x14 -> x16, Pallas kernels: 43.8 us -> 44.8 us  [launch(): pl.pallas_call(body, out_shape=[shape for shape, _ in outputs] + [jax.Sha...]
  transfers between devices with their start and end apart: 17 -> 20, of which waited for: 9 -> 12; matrix products, arithmetic and copies ran while one was open for 0% -> 0% of each run, Pallas kernels for 21% -> 25%
where the time goes in v2:
time: 143 us; the launch traced here: 140 us
  starting transfers between devices  48.9 us (34%)
  Pallas kernels  46.4 us (32%)
  waiting for transfers between devices  39.2 us (27%)
  local copies, waits for them, and re-layouts  4.1 us (3%)
    ppermute x20, starting transfers between devices, work(): send = lambda value, route: lax.ppermute(value, ('gx', 'gy'), routes[route])  48.9 us
    pallas_call x16, Pallas kernels, launch(): pl.pallas_call(body, out_shape=[shape for shape, _ in outputs] + [jax.Sha...  44.8 us
    ppermute x20, waiting for transfers between devices, work(): send = lambda value, route: lax.ppermute(value, ('gx', 'gy'), routes[route])  39.2 us
  transfers between devices with their start and end apart: 20, of which 12 were waited for; matrix products, arithmetic and copies ran while one was open for 0% of the time, Pallas kernels for 25%

profile of v2, /device:TPU:7, one launch (start us, length us, event | category | flops | bytes accessed | tf_op | source)
XLA Modules:
  0.0 140.4 jit_solution(3866065385103899605)
XLA Ops:
  0.6 1.3 copy.58.pairs
  2.0 1.6 %shard_map.77 = (s32[57]{0:T(128)S(1)}, f32[51]{0:T(128)S(1)}) custom-call(s32[3,2]{1,0:T(4,128)} %copy.58.pairs, s32[17]{0:T(128)} %lags.1, f32[4,17]{1,0:T(4,128)} %table.1, s32[3]{0:T(128)} %rows.1), custom_call_target="tpu_custom_call" | custom-call | tf_op jit(solution)/shard_map/pallas_call | solution.py:397
  3.6 0.6 slice.3
  4.8 135.6 %conditional.1 = (f32[3,48,16,256]{3,2,1,0:T(8,128)}, f32[3,48,16,256]{3,2,1,0:T(8,128)}) conditional(s32[]{:T(128)} %bitcast, (s32[57]{0:T(128)S(1)}, f32[4,48,16,256]{3,2,1,0:T(8,128)}, f32[4,48,16,256]{3,2,1,0:T(8,128)}, f32[51]{0:T(128)S(1)}) %tuple.27, (s32[57]{0:T(128)S(1)}, f32[4,48,16,256]{3,2,1,0:T(8,128)}, ...), branch_computations={%region_0.0_spmd, %region_1.0_spmd, %region_2.0_spmd, %region_3.0_... | conditional | bytes 131945752 | solution.py:409
  5.0 0.0 copy-start.13
  5.1 0.0 copy-start.18
  5.1 2.0 %branch_3_fun.16 = (f32[48,16,256]{2,1,0:T(8,128)S(1)}, f32[8,128]{1,0:T(8,128)S(1)}) custom-call(s32[57]{0:T(128)S(1)} %get-tuple-element.142.refs_0_, f32[4,48,16,256]{3,2,1,0:T(8,128)} %get-tuple-element.144.refs_1_, f32[4,48,16,256]{3,2,1,0:T(8,128)} %get-tuple-element.145.refs_2_), custom_call_target="tpu_custom_call" | custom-call | bytes 2000000 | tf_op jit(solution)/shard_map/cond/branch_3_fun/pallas_call | solution.py:82
  7.0 1.4 collective-permute-start.42
  8.4 1.7 %branch_3_fun.17 = (f32[5,48,16,256]{3,2,1,0:T(8,128)S(1)}, f32[5,48,2,256]{3,2,1,0:T(2,128)S(1)}, f32[5,48,2,256]{3,2,1,0:T(2,128)S(1)}, f32[8,128]{1,0:T(8,128)S(1)}) custom-call(s32[57]{0:T(128)S(1)} %get-tuple-element.142.refs_0_, f32[4,48,16,256]{3,2,1,0:T(8,128)S(1)} %copy-done.13, f32[4,48,16,256]{3,2,1,0:T(8,128)S(1)} %copy-done.18, ...), custom_call_target="tpu_custom_call" | custom-call | bytes 2000000 | tf_op jit(solution)/shard_map/cond/branch_3_fun/pallas_call | solution.py:82
  10.1 1.0 collective-permute-start.43
  11.2 4.4 %collective-permute-start.44 = (f32[5,48,2,256]{3,2,1,0:T(2,128)S(1)}, f32[5,48,2,256]{3,2,1,0:T(2,128)S(1)}, u32[]{:S(2)}, u32[]{:S(2)}) collective-permute-start(f32[5,48,2,256]{3,2,1,0:T(2,128)S(1)} %get-tuple-element.151), channel_id=1, source_target_pairs={{1,2},{2,1},{5,6},{6,5},{9,10},{10,9},{13,14},{14,13},{17,18},{18,... | collective-permute-start | bytes 1474568 | tf_op jit(solution)/shard_map/cond/branch_3_fun/ppermute | solution.py:347
  15.6 2.8 %collective-permute-start.45 = (f32[5,48,2,256]{3,2,1,0:T(2,128)S(1)}, f32[5,48,2,256]{3,2,1,0:T(2,128)S(1)}, u32[]{:S(2)}, u32[]{:S(2)}) collective-permute-start(f32[5,48,2,256]{3,2,1,0:T(2,128)S(1)} %get-tuple-element.151), channel_id=1, source_target_pairs={{1,6},{2,5},{5,2},{6,1},{9,14},{10,13},{13,10},{14,9},{17,22},{18,... | collective-permute-start | bytes 1474568 | tf_op jit(solution)/shard_map/cond/branch_3_fun/ppermute | solution.py:347
  18.4 7.7 %collective-permute-start.46 = (f32[5,48,2,256]{3,2,1,0:T(2,128)S(1)}, f32[5,48,2,256]{3,2,1,0:T(2,128)S(1)}, u32[]{:S(2)}, u32[]{:S(2)}) collective-permute-start(f32[5,48,2,256]{3,2,1,0:T(2,128)S(1)} %get-tuple-element.151), channel_id=1, source_target_pairs={{5,10},{6,9},{13,18},{14,17},{21,26},{22,25},{29,34},{30,33},{37,4... | collective-permute-start | bytes 1474568 | tf_op jit(solution)/shard_map/cond/branch_3_fun/ppermute | solution.py:347
  26.1 0.0 collective-permute-done.43.refs_2_.refs_7_.refs_5_
  26.1 14.7 %collective-permute-done.44.refs_3_.refs_8_.refs_6_ = f32[5,48,2,256]{3,2,1,0:T(2,128)S(1)} collective-permute-done((f32[5,48,2,256]{3,2,1,0:T(2,128)S(1)}, f32[5,48,2,256]{3,2,1,0:T(2,128)S(1)}, u32[]{:S(2)}, u32[]{:S(2)}) %collective-permute-start.44) | collective-permute-done | bytes 491552 | tf_op jit(solution)/shard_map/cond/branch_3_fun/ppermute | solution.py:347
  40.8 0.0 collective-permute-done.45.refs_4_.refs_10_.refs_8_
  40.8 0.1 branch_3_fun.18
  40.9 0.1 collective-permute-start.48
  41.0 0.0 collective-permute-done.46.refs_3_.refs_12_.refs_10_
  41.0 0.0 collective-permute-done.42.refs_0_
  41.0 0.1 branch_3_fun.19
  41.1 3.3 %collective-permute-start.50 = (f32[48,16,256]{2,1,0:T(8,128)S(1)}, f32[48,16,256]{2,1,0:T(8,128)S(1)}, u32[]{:S(2)}, u32[]{:S(2)}) collective-permute-start(f32[48,16,256]{2,1,0:T(8,128)S(1)} %get-tuple-element.155.refs_1_.refs_5_), channel_id=1, source_target_pairs={{0,8},{1,9},{2,10},{3,11},{8,16},{9,17},{10,18},{11,19},{16,24},{1... | collective-permute-start | bytes 2359304 | tf_op jit(solution)/shard_map/cond/branch_3_fun/ppermute | solution.py:347
  44.3 3.9 %collective-permute-start.47 = (f32[48,16,256]{2,1,0:T(8,128)S(1)}, f32[48,16,256]{2,1,0:T(8,128)S(1)}, u32[]{:S(2)}, u32[]{:S(2)}) collective-permute-start(f32[48,16,256]{2,1,0:T(8,128)S(1)} %get-tuple-element.153), channel_id=1, source_target_pairs={{0,4},{1,5},{2,6},{3,7},{4,0},{5,1},{6,2},{7,3},{8,12},{9,13},{10,... | collective-permute-start | bytes 2359304 | tf_op jit(solution)/shard_map/cond/branch_3_fun/ppermute | solution.py:347
  48.2 0.6 branch_3_fun.20
  48.9 0.1 collective-permute-start.49
  49.0 1.3 collective-permute-done.49.refs_3_.refs_9_
  50.3 6.7 %collective-permute-done.48.refs_0_ = f32[48,16,256]{2,1,0:T(8,128)S(1)} collective-permute-done((f32[48,16,256]{2,1,0:T(8,128)S(1)}, f32[48,16,256]{2,1,0:T(8,128)S(1)}, u32[]{:S(2)}, u32[]{:S(2)}) %collective-permute-start.48) | collective-permute-done | bytes 786464 | tf_op jit(solution)/shard_map/cond/branch_3_fun/ppermute | solution.py:347
  56.9 0.1 branch_3_fun.21
  57.0 3.8 %collective-permute-start.54 = (f32[48,16,256]{2,1,0:T(8,128)S(1)}, f32[48,16,256]{2,1,0:T(8,128)S(1)}, u32[]{:S(2)}, u32[]{:S(2)}) collective-permute-start(f32[48,16,256]{2,1,0:T(8,128)S(1)} %get-tuple-element.159.refs_1_.refs_5_), channel_id=1, source_target_pairs={{0,8},{1,9},{2,10},{3,11},{8,16},{9,17},{10,18},{11,19},{16,24},{1... | collective-permute-start | bytes 2359304 | tf_op jit(solution)/shard_map/cond/branch_3_fun/ppermute | solution.py:347
  60.9 0.0 collective-permute-done.50.refs_2_.refs_6_
  60.9 0.8 branch_3_fun.22
  61.6 0.1 collective-permute-start.51
  61.7 3.8 %collective-permute-start.53 = (f32[48,16,256]{2,1,0:T(8,128)S(1)}, f32[48,16,256]{2,1,0:T(8,128)S(1)}, u32[]{:S(2)}, u32[]{:S(2)}) collective-permute-start(f32[48,16,256]{2,1,0:T(8,128)S(1)} %get-tuple-element.164), channel_id=1, source_target_pairs={{0,4},{1,5},{2,6},{3,7},{4,0},{5,1},{6,2},{7,3},{8,12},{9,13},{10,... | collective-permute-start | bytes 2359304 | tf_op jit(solution)/shard_map/cond/branch_3_fun/ppermute | solution.py:347
  65.5 0.2 collective-permute-done.47.refs_0_
  65.7 0.0 collective-permute-done.51.refs_3_.refs_11_.refs_9_
  65.7 0.1 branch_3_fun.23
  65.7 4.4 %collective-permute-start.56 = (f32[48,16,256]{2,1,0:T(8,128)S(1)}, f32[48,16,256]{2,1,0:T(8,128)S(1)}, u32[]{:S(2)}, u32[]{:S(2)}) collective-permute-start(f32[48,16,256]{2,1,0:T(8,128)S(1)} %get-tuple-element.165.refs_1_.refs_5_), channel_id=1, source_target_pairs={{0,8},{1,9},{2,10},{3,11},{8,16},{9,17},{10,18},{11,19},{16,24},{1... | collective-permute-start | bytes 2359304 | tf_op jit(solution)/shard_map/cond/branch_3_fun/ppermute | solution.py:347
  70.1 4.4 %collective-permute-start.52 = (f32[48,16,256]{2,1,0:T(8,128)S(1)}, f32[48,16,256]{2,1,0:T(8,128)S(1)}, u32[]{:S(2)}, u32[]{:S(2)}) collective-permute-start(f32[48,16,256]{2,1,0:T(8,128)S(1)} %get-tuple-element.163), channel_id=1, source_target_pairs={{0,4},{1,5},{2,6},{3,7},{4,0},{5,1},{6,2},{7,3},{8,12},{9,13},{10,... | collective-permute-start | bytes 2359304 | tf_op jit(solution)/shard_map/cond/branch_3_fun/ppermute | solution.py:347
  74.6 1.0 collective-permute-done.54.refs_2_.refs_6_
  75.5 11.5 %branch_3_fun.24 = (f32[48,2,512]{2,1,0:T(2,128)S(1)}, f32[3,48,16,256]{3,2,1,0:T(8,128)S(1)}, f32[3,48,16,256]{3,2,1,0:T(8,128)S(1)}, f32[8,128]{1,0:T(8,128)S(1)}) custom-call(s32[57]{0:T(128)S(1)} %get-tuple-element.142.refs_0_, f32[48,16,256]{2,1,0:T(8,128)S(1)} %get-tuple-element.165.refs_1_.refs_5_, ...), custom_call_target="tpu_custom_call" | custom-call | bytes 2000000 | tf_op jit(solution)/shard_map/cond/branch_3_fun/pallas_call | solution.py:82
  87.1 0.1 collective-permute-start.55
  87.2 0.0 collective-permute-done.53.refs_0_
  87.2 1.4 %collective-permute-done.55.refs_2_.refs_11_.refs_9_ = f32[48,2,512]{2,1,0:T(2,128)S(1)} collective-permute-done((f32[48,2,512]{2,1,0:T(2,128)S(1)}, f32[48,2,512]{2,1,0:T(2,128)S(1)}, u32[]{:S(2)}, u32[]{:S(2)}) %collective-permute-start.55) | collective-permute-done | bytes 196640 | tf_op jit(solution)/shard_map/cond/branch_3_fun/ppermute | solution.py:347
  88.6 1.9 %collective-permute-start.59 = (f32[48,16,256]{2,1,0:T(8,128)S(1)}, f32[48,16,256]{2,1,0:T(8,128)S(1)}, u32[]{:S(2)}, u32[]{:S(2)}) collective-permute-start(f32[48,16,256]{2,1,0:T(8,128)S(1)} %get-tuple-element.169.refs_1_.refs_3_), channel_id=1, source_target_pairs={{0,8},{1,9},{2,10},{3,11},{8,16},{9,17},{10,18},{11,19},{16,24},{1... | collective-permute-start | bytes 2359304 | tf_op jit(solution)/shard_map/cond/branch_3_fun/ppermute | solution.py:347
  90.5 0.6 collective-permute-done.56.refs_2_.refs_6_
  91.1 6.8 %branch_3_fun.26 = (f32[48,2,512]{2,1,0:T(2,128)S(1)}, f32[3,48,16,256]{3,2,1,0:T(8,128)S(1)}, f32[3,48,16,256]{3,2,1,0:T(8,128)S(1)}, f32[8,128]{1,0:T(8,128)S(1)}) custom-call(s32[57]{0:T(128)S(1)} %get-tuple-element.142.refs_0_, f32[48,16,256]{2,1,0:T(8,128)S(1)} %get-tuple-element.169.refs_1_.refs_3_, ...), custom_call_target="tpu_custom_call", output_to_operand_aliasing={{1}: (13, {}), {2}: (14, {})} | custom-call | bytes 2000000 | tf_op jit(solution)/shard_map/cond/branch_3_fun/pallas_call | solution.py:82
  97.9 0.1 collective-permute-start.57
  98.0 1.9 %collective-permute-done.52.refs_0_ = f32[48,16,256]{2,1,0:T(8,128)S(1)} collective-permute-done((f32[48,16,256]{2,1,0:T(8,128)S(1)}, f32[48,16,256]{2,1,0:T(8,128)S(1)}, u32[]{:S(2)}, u32[]{:S(2)}) %collective-permute-start.52) | collective-permute-done | bytes 786464 | tf_op jit(solution)/shard_map/cond/branch_3_fun/ppermute | solution.py:347
  99.9 0.0 collective-permute-done.57.refs_2_.refs_11_.refs_7_
  99.9 3.0 %collective-permute-start.58 = (f32[48,16,256]{2,1,0:T(8,128)S(1)}, f32[48,16,256]{2,1,0:T(8,128)S(1)}, u32[]{:S(2)}, u32[]{:S(2)}) collective-permute-start(f32[48,16,256]{2,1,0:T(8,128)S(1)} %get-tuple-element.175.refs_1_.refs_3_), channel_id=1, source_target_pairs={{0,8},{1,9},{2,10},{3,11},{8,16},{9,17},{10,18},{11,19},{16,24},{1... | collective-permute-start | bytes 2359304 | tf_op jit(solution)/shard_map/cond/branch_3_fun/ppermute | solution.py:347
  102.9 8.7 %collective-permute-done.59.refs_2_.refs_4_ = f32[48,16,256]{2,1,0:T(8,128)S(1)} collective-permute-done((f32[48,16,256]{2,1,0:T(8,128)S(1)}, f32[48,16,256]{2,1,0:T(8,128)S(1)}, u32[]{:S(2)}, u32[]{:S(2)}) %collective-permute-start.59) | collective-permute-done | bytes 786464 | tf_op jit(solution)/shard_map/cond/branch_3_fun/ppermute | solution.py:347
  111.6 6.8 %branch_3_fun.28 = (f32[48,2,512]{2,1,0:T(2,128)S(1)}, f32[3,48,16,256]{3,2,1,0:T(8,128)S(1)}, f32[3,48,16,256]{3,2,1,0:T(8,128)S(1)}, f32[8,128]{1,0:T(8,128)S(1)}) custom-call(s32[57]{0:T(128)S(1)} %get-tuple-element.142.refs_0_, f32[48,16,256]{2,1,0:T(8,128)S(1)} %get-tuple-element.175.refs_1_.refs_3_, ...), custom_call_target="tpu_custom_call", output_to_operand_aliasing={{1}: (13, {}), {2}: (14, {})} | custom-call | bytes 2000000 | tf_op jit(solution)/shard_map/cond/branch_3_fun/pallas_call | solution.py:82
  118.4 1.6 %collective-permute-start.60 = (f32[48,2,512]{2,1,0:T(2,128)S(1)}, f32[48,2,512]{2,1,0:T(2,128)S(1)}, u32[]{:S(2)}, u32[]{:S(2)}) collective-permute-start(f32[48,2,512]{2,1,0:T(2,128)S(1)} %get-tuple-element.179), channel_id=1, source_target_pairs={{0,1},{1,0},{2,3},{3,2},{4,5},{5,4},{6,7},{7,6},{8,9},{9,8},{10,11... | collective-permute-start | bytes 589832 | tf_op jit(solution)/shard_map/cond/branch_3_fun/ppermute | solution.py:347
  120.0 1.1 collective-permute-done.60.refs_9_.refs_7_
  121.1 6.6 %branch_3_fun.29 = (f32[3,48,16,256]{3,2,1,0:T(8,128)S(1)}, f32[3,48,16,256]{3,2,1,0:T(8,128)S(1)}, f32[8,128]{1,0:T(8,128)S(1)}) custom-call(s32[57]{0:T(128)S(1)} %get-tuple-element.142.refs_0_, f32[51]{0:T(128)S(1)} %get-tuple-element.143.refs_3_.refs_1_, ...), custom_call_target="tpu_custom_call", output_to_operand_aliasing={{0}: (11, {}), {1}: (12, {})} | custom-call | bytes 2000000 | tf_op jit(solution)/shard_map/cond/branch_3_fun/pallas_call | solution.py:82
  127.6 0.8 collective-permute-done.58.refs_1_.refs_4_
  128.5 0.6 branch_3_fun.30
  129.1 1.0 collective-permute-start.61
  130.2 0.9 collective-permute-done.61.refs_9_
  131.1 7.1 %branch_3_fun.31 = (f32[3,48,16,256]{3,2,1,0:T(8,128)S(1)}, f32[3,48,16,256]{3,2,1,0:T(8,128)S(1)}, f32[8,128]{1,0:T(8,128)}) custom-call(s32[57]{0:T(128)S(1)} %get-tuple-element.142.refs_0_, f32[51]{0:T(128)S(1)} %get-tuple-element.143.refs_3_.refs_1_, ...), custom_call_target="tpu_custom_call", output_to_operand_aliasing={{0}: (11, {}), {1}: (12, {})} | custom-call | bytes 2000000 | tf_op jit(solution)/shard_map/cond/branch_3_fun/pallas_call | solution.py:82
  138.3 0.0 copy-start.3
  138.3 0.0 copy-start.8
  138.3 1.4 copy-done.3
  139.7 0.8 copy-done.8
  (4 shorter events, 0.0 us)
Async XLA Ops:
  5.0 3.4 %copy-start.13 = (f32[4,48,16,256]{3,2,1,0:T(8,128)S(1)}, f32[4,48,16,256]{3,2,1,0:T(8,128)}, u32[]{:S(2)}) copy-start(f32[4,48,16,256]{3,2,1,0:T(8,128)} %get-tuple-element.144.refs_1_) | copy-start | bytes 9437188 | tf_op jit(solution)/shard_map/cond
  5.1 3.4 %copy-start.18 = (f32[4,48,16,256]{3,2,1,0:T(8,128)S(1)}, f32[4,48,16,256]{3,2,1,0:T(8,128)}, u32[]{:S(2)}) copy-start(f32[4,48,16,256]{3,2,1,0:T(8,128)} %get-tuple-element.145.refs_2_) | copy-start | bytes 9437188 | tf_op jit(solution)/shard_map/cond
  7.0 34.0 %collective-permute-start.42 = (f32[48,16,256]{2,1,0:T(8,128)S(1)}, f32[48,16,256]{2,1,0:T(8,128)S(1)}, u32[]{:S(2)}, u32[]{:S(2)}) collective-permute-start(f32[48,16,256]{2,1,0:T(8,128)S(1)} %get-tuple-element.148), channel_id=1, source_target_pairs={{0,4},{1,5},{2,6},{3,7},{4,0},{5,1},{6,2},{7,3},{8,12},{9,13},{10,... | collective-permute-start | bytes 2359304 | tf_op jit(solution)/shard_map/cond/branch_3_fun/ppermute | solution.py:347
  10.1 16.0 %collective-permute-start.43 = (f32[5,48,2,256]{3,2,1,0:T(2,128)S(1)}, f32[5,48,2,256]{3,2,1,0:T(2,128)S(1)}, u32[]{:S(2)}, u32[]{:S(2)}) collective-permute-start(f32[5,48,2,256]{3,2,1,0:T(2,128)S(1)} %get-tuple-element.150), channel_id=1, source_target_pairs={{0,1},{1,0},{2,3},{3,2},{4,5},{5,4},{6,7},{7,6},{8,9},{9,8},{10,11... | collective-permute-start | bytes 1474568 | tf_op jit(solution)/shard_map/cond/branch_3_fun/ppermute | solution.py:347
  11.2 29.7 %collective-permute-start.44 = (f32[5,48,2,256]{3,2,1,0:T(2,128)S(1)}, f32[5,48,2,256]{3,2,1,0:T(2,128)S(1)}, u32[]{:S(2)}, u32[]{:S(2)}) collective-permute-start(f32[5,48,2,256]{3,2,1,0:T(2,128)S(1)} %get-tuple-element.151), channel_id=1, source_target_pairs={{1,2},{2,1},{5,6},{6,5},{9,10},{10,9},{13,14},{14,13},{17,18},{18,... | collective-permute-start | bytes 1474568 | tf_op jit(solution)/shard_map/cond/branch_3_fun/ppermute | solution.py:347
  15.6 25.2 %collective-permute-start.45 = (f32[5,48,2,256]{3,2,1,0:T(2,128)S(1)}, f32[5,48,2,256]{3,2,1,0:T(2,128)S(1)}, u32[]{:S(2)}, u32[]{:S(2)}) collective-permute-start(f32[5,48,2,256]{3,2,1,0:T(2,128)S(1)} %get-tuple-element.151), channel_id=1, source_target_pairs={{1,6},{2,5},{5,2},{6,1},{9,14},{10,13},{13,10},{14,9},{17,22},{18,... | collective-permute-start | bytes 1474568 | tf_op jit(solution)/shard_map/cond/branch_3_fun/ppermute | solution.py:347
  18.4 22.6 %collective-permute-start.46 = (f32[5,48,2,256]{3,2,1,0:T(2,128)S(1)}, f32[5,48,2,256]{3,2,1,0:T(2,128)S(1)}, u32[]{:S(2)}, u32[]{:S(2)}) collective-permute-start(f32[5,48,2,256]{3,2,1,0:T(2,128)S(1)} %get-tuple-element.151), channel_id=1, source_target_pairs={{5,10},{6,9},{13,18},{14,17},{21,26},{22,25},{29,34},{30,33},{37,4... | collective-permute-start | bytes 1474568 | tf_op jit(solution)/shard_map/cond/branch_3_fun/ppermute | solution.py:347
  40.9 16.0 %collective-permute-start.48 = (f32[48,16,256]{2,1,0:T(8,128)S(1)}, f32[48,16,256]{2,1,0:T(8,128)S(1)}, u32[]{:S(2)}, u32[]{:S(2)}) collective-permute-start(f32[48,16,256]{2,1,0:T(8,128)S(1)} %get-tuple-element.154), channel_id=1, source_target_pairs={{0,4},{1,5},{2,6},{3,7},{4,0},{5,1},{6,2},{7,3},{8,12},{9,13},{10,... | collective-permute-start | bytes 2359304 | tf_op jit(solution)/shard_map/cond/branch_3_fun/ppermute | solution.py:347
  41.1 19.8 %collective-permute-start.50 = (f32[48,16,256]{2,1,0:T(8,128)S(1)}, f32[48,16,256]{2,1,0:T(8,128)S(1)}, u32[]{:S(2)}, u32[]{:S(2)}) collective-permute-start(f32[48,16,256]{2,1,0:T(8,128)S(1)} %get-tuple-element.155.refs_1_.refs_5_), channel_id=1, source_target_pairs={{0,8},{1,9},{2,10},{3,11},{8,16},{9,17},{10,18},{11,19},{16,24},{1... | collective-permute-start | bytes 2359304 | tf_op jit(solution)/shard_map/cond/branch_3_fun/ppermute | solution.py:347
  44.3 21.3 %collective-permute-start.47 = (f32[48,16,256]{2,1,0:T(8,128)S(1)}, f32[48,16,256]{2,1,0:T(8,128)S(1)}, u32[]{:S(2)}, u32[]{:S(2)}) collective-permute-start(f32[48,16,256]{2,1,0:T(8,128)S(1)} %get-tuple-element.153), channel_id=1, source_target_pairs={{0,4},{1,5},{2,6},{3,7},{4,0},{5,1},{6,2},{7,3},{8,12},{9,13},{10,... | collective-permute-start | bytes 2359304 | tf_op jit(solution)/shard_map/cond/branch_3_fun/ppermute | solution.py:347
  48.9 1.4 collective-permute-start.49
  57.0 18.5 %collective-permute-start.54 = (f32[48,16,256]{2,1,0:T(8,128)S(1)}, f32[48,16,256]{2,1,0:T(8,128)S(1)}, u32[]{:S(2)}, u32[]{:S(2)}) collective-permute-start(f32[48,16,256]{2,1,0:T(8,128)S(1)} %get-tuple-element.159.refs_1_.refs_5_), channel_id=1, source_target_pairs={{0,8},{1,9},{2,10},{3,11},{8,16},{9,17},{10,18},{11,19},{16,24},{1... | collective-permute-start | bytes 2359304 | tf_op jit(solution)/shard_map/cond/branch_3_fun/ppermute | solution.py:347
  61.6 4.0 %collective-permute-start.51 = (f32[48,2,512]{2,1,0:T(2,128)S(1)}, f32[48,2,512]{2,1,0:T(2,128)S(1)}, u32[]{:S(2)}, u32[]{:S(2)}) collective-permute-start(f32[48,2,512]{2,1,0:T(2,128)S(1)} %get-tuple-element.162), channel_id=1, source_target_pairs={{0,1},{1,0},{2,3},{3,2},{4,5},{5,4},{6,7},{7,6},{8,9},{9,8},{10,11... | collective-permute-start | bytes 589832 | tf_op jit(solution)/shard_map/cond/branch_3_fun/ppermute | solution.py:347
  61.7 25.5 %collective-permute-start.53 = (f32[48,16,256]{2,1,0:T(8,128)S(1)}, f32[48,16,256]{2,1,0:T(8,128)S(1)}, u32[]{:S(2)}, u32[]{:S(2)}) collective-permute-start(f32[48,16,256]{2,1,0:T(8,128)S(1)} %get-tuple-element.164), channel_id=1, source_target_pairs={{0,4},{1,5},{2,6},{3,7},{4,0},{5,1},{6,2},{7,3},{8,12},{9,13},{10,... | collective-permute-start | bytes 2359304 | tf_op jit(solution)/shard_map/cond/branch_3_fun/ppermute | solution.py:347
  65.7 25.4 %collective-permute-start.56 = (f32[48,16,256]{2,1,0:T(8,128)S(1)}, f32[48,16,256]{2,1,0:T(8,128)S(1)}, u32[]{:S(2)}, u32[]{:S(2)}) collective-permute-start(f32[48,16,256]{2,1,0:T(8,128)S(1)} %get-tuple-element.165.refs_1_.refs_5_), channel_id=1, source_target_pairs={{0,8},{1,9},{2,10},{3,11},{8,16},{9,17},{10,18},{11,19},{16,24},{1... | collective-permute-start | bytes 2359304 | tf_op jit(solution)/shard_map/cond/branch_3_fun/ppermute | solution.py:347
  70.1 29.8 %collective-permute-start.52 = (f32[48,16,256]{2,1,0:T(8,128)S(1)}, f32[48,16,256]{2,1,0:T(8,128)S(1)}, u32[]{:S(2)}, u32[]{:S(2)}) collective-permute-start(f32[48,16,256]{2,1,0:T(8,128)S(1)} %get-tuple-element.163), channel_id=1, source_target_pairs={{0,4},{1,5},{2,6},{3,7},{4,0},{5,1},{6,2},{7,3},{8,12},{9,13},{10,... | collective-permute-start | bytes 2359304 | tf_op jit(solution)/shard_map/cond/branch_3_fun/ppermute | solution.py:347
  87.1 1.5 %collective-permute-start.55 = (f32[48,2,512]{2,1,0:T(2,128)S(1)}, f32[48,2,512]{2,1,0:T(2,128)S(1)}, u32[]{:S(2)}, u32[]{:S(2)}) collective-permute-start(f32[48,2,512]{2,1,0:T(2,128)S(1)} %get-tuple-element.168), channel_id=1, source_target_pairs={{0,1},{1,0},{2,3},{3,2},{4,5},{5,4},{6,7},{7,6},{8,9},{9,8},{10,11... | collective-permute-start | bytes 589832 | tf_op jit(solution)/shard_map/cond/branch_3_fun/ppermute | solution.py:347
  88.6 23.0 %collective-permute-start.59 = (f32[48,16,256]{2,1,0:T(8,128)S(1)}, f32[48,16,256]{2,1,0:T(8,128)S(1)}, u32[]{:S(2)}, u32[]{:S(2)}) collective-permute-start(f32[48,16,256]{2,1,0:T(8,128)S(1)} %get-tuple-element.169.refs_1_.refs_3_), channel_id=1, source_target_pairs={{0,8},{1,9},{2,10},{3,11},{8,16},{9,17},{10,18},{11,19},{16,24},{1... | collective-permute-start | bytes 2359304 | tf_op jit(solution)/shard_map/cond/branch_3_fun/ppermute | solution.py:347
  97.9 2.0 %collective-permute-start.57 = (f32[48,2,512]{2,1,0:T(2,128)S(1)}, f32[48,2,512]{2,1,0:T(2,128)S(1)}, u32[]{:S(2)}, u32[]{:S(2)}) collective-permute-start(f32[48,2,512]{2,1,0:T(2,128)S(1)} %get-tuple-element.174), channel_id=1, source_target_pairs={{0,1},{1,0},{2,3},{3,2},{4,5},{5,4},{6,7},{7,6},{8,9},{9,8},{10,11... | collective-permute-start | bytes 589832 | tf_op jit(solution)/shard_map/cond/branch_3_fun/ppermute | solution.py:347
  99.9 28.6 %collective-permute-start.58 = (f32[48,16,256]{2,1,0:T(8,128)S(1)}, f32[48,16,256]{2,1,0:T(8,128)S(1)}, u32[]{:S(2)}, u32[]{:S(2)}) collective-permute-start(f32[48,16,256]{2,1,0:T(8,128)S(1)} %get-tuple-element.175.refs_1_.refs_3_), channel_id=1, source_target_pairs={{0,8},{1,9},{2,10},{3,11},{8,16},{9,17},{10,18},{11,19},{16,24},{1... | collective-permute-start | bytes 2359304 | tf_op jit(solution)/shard_map/cond/branch_3_fun/ppermute | solution.py:347
  118.4 2.7 %collective-permute-start.60 = (f32[48,2,512]{2,1,0:T(2,128)S(1)}, f32[48,2,512]{2,1,0:T(2,128)S(1)}, u32[]{:S(2)}, u32[]{:S(2)}) collective-permute-start(f32[48,2,512]{2,1,0:T(2,128)S(1)} %get-tuple-element.179), channel_id=1, source_target_pairs={{0,1},{1,0},{2,3},{3,2},{4,5},{5,4},{6,7},{7,6},{8,9},{9,8},{10,11... | collective-permute-start | bytes 589832 | tf_op jit(solution)/shard_map/cond/branch_3_fun/ppermute | solution.py:347
  129.1 2.0 %collective-permute-start.61 = (f32[48,2,256]{2,1,0:T(2,128)S(1)}, f32[48,2,256]{2,1,0:T(2,128)S(1)}, u32[]{:S(2)}, u32[]{:S(2)}) collective-permute-start(f32[48,2,256]{2,1,0:T(2,128)S(1)} %get-tuple-element.184), channel_id=1, source_target_pairs={{0,1},{1,0},{2,3},{3,2},{4,5},{5,4},{6,7},{7,6},{8,9},{9,8},{10,11... | collective-permute-start | bytes 294920 | tf_op jit(solution)/shard_map/cond/branch_3_fun/ppermute | solution.py:347
  138.3 1.4 %copy-start.3 = (f32[3,48,16,256]{3,2,1,0:T(8,128)}, f32[3,48,16,256]{3,2,1,0:T(8,128)S(1)}, u32[]{:S(2)}) copy-start(f32[3,48,16,256]{3,2,1,0:T(8,128)S(1)} %get-tuple-element.257) | copy-start | bytes 7077892 | tf_op jit(solution)/shard_map/cond
  138.3 2.2 %copy-start.8 = (f32[3,48,16,256]{3,2,1,0:T(8,128)}, f32[3,48,16,256]{3,2,1,0:T(8,128)S(1)}, u32[]{:S(2)}) copy-start(f32[3,48,16,256]{3,2,1,0:T(8,128)S(1)} %get-tuple-element.258) | copy-start | bytes 7077892 | tf_op jit(solution)/shard_map/cond
